TPU v7x, 128 devices: a whole 4x4x4 slice. The times are simulated.
128 devices in a mesh: grid: 16 (over z, x_hi, core), pair: 8 (over y, x_lo).
Axes of the slice: x: 4 (x_hi: 2, x_lo: 2; x = x_hi * 2 + x_lo), y: 4, z: 4, core: 2. Of those that a mesh axis runs over, the one named last changes fastest.
Arguments:
- amplitudes: bfloat16 [8, 1500, 1500], P('pair'), may hold values from -6 to 6
- factors: bfloat16 [1500, 6000], P(None, 'grid'), may hold values from -0.15625 to 0.15625
- z_values: bfloat16 [6000, 6000], P('grid', 'pair'), may hold values from -6 to 6
- z_scales: float32 [48, 48], P('grid', 'pair'), may hold values from 0.3 to 3
- pair_index: int32 [8], P('pair'), may hold values from 0 to 11174
- vir_energy: float32 [1500], replicated, may hold values from 0.5 to 2.5
- occ_energy: float32 [150], replicated, may hold values from -4 to -0.5
Outputs:
- update: float32 [8, 2250000], P('pair', 'grid')
All inputs are finite; a program needn't handle non-finite values.
Results may differ from a plain program's by a relative error of at most 0.004.
Values may be sent and summed in bfloat16 or wider, within the bound.
No kernel may reach another device: no remote copies, remote signals or barrier semaphores. Data moves between devices by JAX's collectives and lax.ppermute only.
A program may use at most 128 MiB of HBM per device.

v0:
```python
import itertools

import jax
import jax.numpy as jnp
from jax import lax
from jax.experimental import pallas as pl
from jax.experimental.pallas import tpu as pltpu
from jax.sharding import PartitionSpec as P

VIRT = 1500
ZBLK = 125
BLK = 375
BPAD = 384
TWO = 2 * BPAD
VPAD = 1536
WIN = 96
BOTH = ("grid", "pair")
ALL = list(itertools.product(range(4), range(4), range(2), range(4)))
F32 = jnp.float32
BF16 = jnp.bfloat16


def flat_index(z, x, c, y):
    return ((z % 4) * 4 + (x % 4) // 2 * 2 + c % 2) * 8 + (y % 4) * 2 + (x % 4) % 2


def move(block, target):
    pairs = []
    for z, x, c, y in ALL:
        dest = target(z, x, c, y)
        if dest is not None:
            pairs.append((flat_index(z, x, c, y), flat_index(*dest)))
    return lax.ppermute(block, BOTH, pairs)


def across(block):
    return move(block, lambda z, x, c, y: (z, x, 1 - c, y))


def dot(a, b, contract_a, contract_b):
    return lax.dot_general(
        a, b, (((contract_a,), (contract_b,)), ((), ())), preferred_element_type=F32
    )


VMEM = pl.BlockSpec(memory_space=pltpu.VMEM)
SMEM = pl.BlockSpec(memory_space=pltpu.SMEM)
HBM = pl.BlockSpec(memory_space=pl.ANY)


def call(kernel, out_shape, scratch, *args, in_specs=None, out_specs=None, mib=20, weight=0):
    many = isinstance(out_shape, (tuple, list))
    return pl.pallas_call(
        kernel,
        out_shape=out_shape,
        in_specs=in_specs or [VMEM] * len(args),
        out_specs=out_specs or (tuple([VMEM] * len(out_shape)) if many else VMEM),
        scratch_shapes=scratch,
        cost_estimate=pl.CostEstimate(flops=1 + weight * 10**9, bytes_accessed=1 + weight * 10**6, transcendentals=0),
        compiler_params=pltpu.CompilerParams(vmem_limit_bytes=mib * 2**20),
    )(*args)


def pad_metric(z_hbm, s_ref, z_out, tmp, z_ref, sem):
    load = pltpu.make_async_copy(z_hbm, z_ref, sem)
    load.start()
    tmp[...] = jnp.zeros_like(tmp)
    load.wait()
    z = z_ref[...].astype(F32)
    tmp[:BLK, :BLK] = z[:, :BLK]
    tmp[:BLK, BPAD : BPAD + BLK] = z[:, BLK:]
    lane = lax.broadcasted_iota(jnp.int32, (1, TWO), 1)
    for r in range(3):
        row = jnp.zeros((1, TWO), F32)
        for q in range(6):
            start = (q // 3) * BPAD + (q % 3) * ZBLK
            row = jnp.where((lane >= start) & (lane < start + ZBLK), s_ref[r, q], row)
        for part in range(3):
            piece = row.astype(BF16).astype(F32)
            tmp[BLK + 3 * part + r : BLK + 3 * part + r + 1, :] = piece
            row = row - piece
    z_out[...] = tmp[...].astype(BF16)


def pad_factors(own_ref, pair_ref, both_out, own_out):
    both_out[...] = jnp.zeros_like(both_out)
    both_out[0, :VIRT, :BLK] = own_ref[...]
    both_out[1, :VIRT, :BLK] = pair_ref[...]
    own_out[...] = jnp.zeros_like(own_out)
    own_out[:VIRT, :BLK] = own_ref[...]


def scaled(block):
    z = block.astype(F32)
    tail = z[BPAD - 16 :, :]
    parts = [tail[7 + r : 8 + r] + tail[10 + r : 11 + r] + tail[13 + r : 14 + r] for r in range(3)]
    row = lax.broadcasted_iota(jnp.int32, (BPAD, 1), 0)
    scale = jnp.where(row < ZBLK, parts[0], jnp.where(row < 2 * ZBLK, parts[1], parts[2]))
    return jnp.where(row < BLK, z * scale, 0.0)


def half(info, x_ref, amp_ref, h_ref, w_ref, xf):
    if x_ref.shape != xf.shape:
        xf[...] = jnp.zeros_like(xf)
    xf[: x_ref.shape[0], : x_ref.shape[1]] = x_ref[...].astype(F32)
    for c in range(2):
        for chip in range(8):
            start = (chip * 2 + c) * BLK // 4
            w_ref[info[2 + c], info[8 + chip]] = xf[start : start + WIN, :].astype(BF16)
    h_ref[...] = jnp.zeros_like(h_ref)
    h_ref[:, :VIRT] = dot(xf[...].T.astype(BF16)[:, :VIRT], amp_ref[0], 1, 0).astype(BF16)


def copy_whole(in_ref, o_ref):
    o_ref[...] = in_ref[...]


def choose_rows(info, own_ref, a_ref, b_ref, o_ref):
    @pl.when(info[1] == 1)
    def _():
        o_ref[0] = own_ref[...]
        o_ref[1] = a_ref[...]

    @pl.when(info[1] == 0)
    def _():
        o_ref[0] = a_ref[...]
        o_ref[1] = b_ref[...]


def choose_onward(info, first_ref, second_ref, o_ref):
    @pl.when(info[0] == 0)
    def _():
        o_ref[...] = first_ref[...]

    @pl.when(info[0] == 1)
    def _():
        o_ref[...] = second_ref[...]


class Factors:
    def __init__(self, info, step, x_refs, slot, first_col, sems):
        own, near, swapped, far, far_pair = x_refs
        self.info, self.step, self.sems = info, step, sems
        self.slot, self.first_col = slot, first_col
        self.sources = {
            (0, 0): (own.at[0], own.at[1]),
            (0, 1): (own.at[1], own.at[0]),
            (1, 0): (swapped.at[1], swapped.at[0]),
            (1, 1): (near.at[1], near.at[0]),
            (2, 0): (far, far_pair),
            (2, 1): (far_pair, far),
            (3, 0): (near.at[0], near.at[1]),
            (3, 1): (swapped.at[0], swapped.at[1]),
        }

    def copy(self, ref, side):
        to = self.slot.at[:, pl.ds(self.first_col + side * BPAD, BPAD)]
        return pltpu.make_async_copy(ref, to, self.sems.at[side])

    def start(self):
        for (place, core), refs in self.sources.items():

            @pl.when((self.info[4 + self.step] == place) & (self.info[0] == core))
            def _():
                for side in range(2):
                    self.copy(refs[side], side).start()

    def wait(self):
        for side in range(2):
            self.copy(self.sources[2, 0][side], side).wait()


def weigh(h_ref, x, z):
    return (dot(h_ref[...], x, 1, 0) * scaled(z)).astype(BF16)


def early_blocks(info, h0_ref, h1_ref, *refs):
    x_refs, z_refs, back_out = refs[:5], refs[5:8], refs[8]
    xs, zs, xsem, zsem = refs[9:]
    for i in range(3):
        Factors(info, i, x_refs, xs.at[i], 0, xsem.at[i]).start()
        pltpu.make_async_copy(z_refs[i], zs.at[i], zsem.at[i]).start()
    back_out[...] = jnp.zeros_like(back_out)

    def block(i, carry):
        Factors(info, i, x_refs, xs.at[i], 0, xsem.at[i]).wait()
        pltpu.make_async_copy(z_refs[0], zs.at[i], zsem.at[i]).wait()
        for b, h_ref in enumerate((h0_ref, h1_ref)):
            rows = slice(b * BPAD, b * BPAD + BPAD)
            x = xs[i]
            back_out[rows, :] += dot(weigh(h_ref, x, zs[i, b]), x, 1, 1)
        return carry

    lax.fori_loop(0, 3, block, 0)


def window_loads(side, w0_ref, w1_ref, left, sems):
    loads = [
        pltpu.make_async_copy(w_ref.at[side], left.at[:, :, pl.ds(b * BPAD, BPAD)], sems.at[b])
        for b, w_ref in enumerate((w0_ref, w1_ref))
    ]
    for load in loads:
        load.start()
    return loads


def give_half(left_loads, left, back, give_ref):
    for load in left_loads:
        load.wait()
    give_ref[...] = dot(left[...].reshape(8 * WIN, TWO), back, 1, 0).astype(BF16)


def last_block(info, h0_ref, h1_ref, *refs):
    x_refs, z_ref, early_ref, w0_ref, w1_ref = refs[:5], *refs[5:9]
    w_out, xn_out, back_out, give_ref, left, xsem, vsem = refs[9:]
    newest = Factors(info, 3, x_refs, xn_out, 0, xsem)
    newest.start()
    left_loads = window_loads(0, w0_ref, w1_ref, left, vsem)
    newest.wait()
    for b, h_ref in enumerate((h0_ref, h1_ref)):
        w_out[b * BPAD : b * BPAD + BPAD, :] = weigh(h_ref, xn_out[...], z_ref[b])
    part = dot(w_out[...], xn_out[:TWO, :], 1, 1)
    back_out[...] = (early_ref[:, :TWO] + part).astype(BF16)
    give_half(left_loads, left, back_out[...], give_ref)


def second_half(early_ref, newest_ref, xn_ref, w0_ref, w1_ref, back_out, give_ref, left, vsem):
    left_loads = window_loads(0, w0_ref, w1_ref, left, vsem)
    part = dot(newest_ref[...], xn_ref[TWO:, :], 1, 1)
    back_out[...] = (early_ref[:, TWO:] + part).astype(BF16)
    give_half(left_loads, left, back_out[...], give_ref)


def keep_sum(back_ref, w0_ref, w1_ref, got_ref, left, vsem):
    for load in window_loads(1, w0_ref, w1_ref, left, vsem):
        load.wait()
    return dot(left[...].reshape(8 * WIN, TWO), back_ref[...], 1, 0) + got_ref[...].astype(F32)


def keep_x(back_ref, w0_ref, w1_ref, got_ref, own_ref, send_ref, left, vsem):
    total = keep_sum(back_ref, w0_ref, w1_ref, got_ref, left, vsem)
    own_ref[...] = total[: 4 * WIN]
    send_ref[...] = total[4 * WIN :].astype(BF16)


def keep_z(back_ref, w0_ref, w1_ref, got_ref, own_ref, *refs):
    send_refs, left, vsem = refs[:3], refs[3], refs[4]
    total = keep_sum(back_ref, w0_ref, w1_ref, got_ref, left, vsem)
    for dx in range(2):
        for dz in range(4):
            part = total[(4 * dx + dz) * WIN : (4 * dx + dz + 1) * WIN]
            if dz == 0:
                own_ref[dx] = part
            else:
                send_refs[dz - 1][dx] = part.astype(BF16)


def then_z(own_ref, got_ref, out_ref, *send_refs):
    total = own_ref[...] + got_ref[...].astype(F32)
    out_ref[...] = total[:WIN]
    for dz in range(1, 4):
        send_refs[dz - 1][...] = total[dz * WIN : (dz + 1) * WIN].astype(BF16)


def then_x(own_ref, got_1, got_2, got_3, out_ref, send_ref):
    total = own_ref[...] + got_1[...].astype(F32) + got_2[...].astype(F32) + got_3[...].astype(F32)
    out_ref[...] = total[0]
    send_ref[...] = total[1].astype(BF16)


def add_parts(own_ref, *refs):
    o_ref = refs[-1]
    total = own_ref[...]
    for ref in refs[:-1]:
        total = total + ref[...].astype(F32)
    o_ref[...] = total


def finish(numbers, occ_ref, vir_ref, a_ref, b_ref, b1_ref, o_ref, out):
    packed, first_row, first_cell = numbers[0], numbers[1], numbers[2]
    count = occ_ref.shape[1]
    orbital = lax.broadcasted_iota(jnp.int32, (1, count), 1)
    starts = orbital * (2 * count - orbital - 1) // 2
    first_occ = jnp.sum(((starts <= packed) & (orbital > 0)).astype(jnp.int32))
    second_occ = packed - first_occ * (2 * count - first_occ - 1) // 2 + first_occ + 1
    occ = jnp.where(orbital == first_occ, occ_ref[...], 0.0)
    occ = occ + jnp.where(orbital == second_occ, occ_ref[...], 0.0)
    row = lax.broadcasted_iota(jnp.int32, (WIN, VIRT), 0) + first_row
    column = lax.broadcasted_iota(jnp.int32, (WIN, VIRT), 1)
    vir = vir_ref[...]
    vir_rows = jnp.sum(jnp.where(row == column, vir, 0.0), axis=1, keepdims=True)
    vir_rows = jnp.where(row[:, :1] < VIRT, vir_rows, 1.0)
    gaps = vir_rows + vir - jnp.sum(occ, axis=1, keepdims=True)
    out[:, :TWO] = a_ref[...] / gaps[:, :TWO]
    total_b = b_ref[...] + b1_ref[...].astype(F32)
    out[:, TWO:] = total_b[:, : VIRT - TWO] / gaps[:, TWO:]
    rows = o_ref.shape[0]
    for shift in range(0, VIRT, BLK):

        @pl.when(first_cell == shift)
        def _():
            if shift == 0:
                o_ref[...] = out[:rows, :]
            else:
                o_ref[:, : VIRT - shift] = out[:rows, shift:]
                o_ref[:, VIRT - shift :] = out[1 : rows + 1, :shift]


def shape(*dims, dtype=BF16):
    return jax.ShapeDtypeStruct(dims, dtype)


def local(amplitudes, factors, z_values, z_scales, pair_index, vir_energy, occ_energy):
    grid_pos = lax.axis_index("grid")
    pair_pos = lax.axis_index("pair")
    z_pos = grid_pos // 4
    x_hi = (grid_pos // 2) % 2
    core = grid_pos % 2
    y_pos = pair_pos // 2
    x_pos = 2 * x_hi + pair_pos % 2
    outer = (x_pos == 0) | (x_pos == 3)
    order = [(y_pos + i - z_pos) % 4 for i in (0, 1, 3, 2)]
    places = [(chip // 2 - z_pos) % 4 + 4 * ((chip % 2 - x_hi) % 2) for chip in range(8)]
    info = jnp.stack([core, outer.astype(jnp.int32), 1 - core, core] + order + places).astype(jnp.int32)

    theirs = across(factors)
    z_own = call(
        pad_metric,
        shape(BPAD, TWO),
        [
            pltpu.VMEM((BPAD, TWO), F32),
            pltpu.VMEM((BLK, 2 * BLK), BF16),
            pltpu.SemaphoreType.DMA,
        ],
        z_values,
        z_scales,
        in_specs=[HBM, SMEM],
        mib=60,
    )
    hop_a = {0: 1, 3: 2, 2: 0, 1: 3}
    hop_b = {2: 1, 1: 2}
    recv_a = move(z_own, lambda z, x, c, y: (z, hop_a[x], c, y))
    recv_b = move(z_own, lambda z, x, c, y: (z, hop_b[x], c, y) if x in hop_b else None)
    theirs, z_own = lax.optimization_barrier((theirs, z_own))
    x_pair, x_own = call(
        pad_factors, (shape(2, VPAD, BPAD), shape(VPAD, BPAD)), [], factors, theirs
    )

    def halves_of(block, amp, weight=0):
        return call(
            half,
            (shape(BPAD, VPAD), shape(2, 8, WIN, BPAD)),
            [pltpu.VMEM((VPAD, BPAD), F32)],
            info,
            block,
            amp,
            in_specs=[SMEM, VMEM, VMEM],
            weight=weight,
        )

    half_0, wins_0 = halves_of(x_own, amplitudes)
    onward = lambda z, x, c, y: (z + 1 - 2 * c, x, c, y)
    near = move(x_pair, onward)
    recv_a, recv_b, half_0, x_again = lax.optimization_barrier((recv_a, recv_b, half_0, x_own))
    x_other = move(x_again, lambda z, x, c, y: (z, 3 - x, c, y))
    z_here = call(
        choose_rows,
        shape(2, BPAD, TWO),
        [],
        info,
        z_own,
        recv_a,
        recv_b,
        in_specs=[SMEM] + [VMEM] * 3,
        weight=20,
    )
    z_before = move(z_here, lambda z, x, c, y: (z, x, c, y + 1))
    z_after = move(z_here, lambda z, x, c, y: (z, x, c, y - 1))
    far = move(near[0], onward)
    amp_later, far_source = lax.optimization_barrier((amplitudes, near))
    amp_again = call(copy_whole, shape(1, VIRT, VIRT), [], amp_later)
    x_other, amp_again = lax.optimization_barrier((x_other, amp_again))
    half_1, wins_1 = halves_of(x_other, amp_again, 10)
    z_before, z_after, half_1 = lax.optimization_barrier((z_before, z_after, half_1))
    z_onward = call(
        choose_onward,
        shape(2, BPAD, TWO),
        [],
        info,
        z_before,
        z_after,
        in_specs=[SMEM] + [VMEM] * 2,
    )
    z_far = move(z_onward, lambda z, x, c, y: (z, x, c, y + 1 - 2 * c))
    far, _ = lax.optimization_barrier((far, z_onward))
    x_parts = [x_pair, near, across(near), far, across(far)]
    dma = pltpu.SemaphoreType.DMA
    early = call(
        early_blocks,
        shape(TWO, VPAD, dtype=F32),
        [
            pltpu.VMEM((3, VPAD, TWO), BF16),
            pltpu.VMEM((3, 2, BPAD, TWO), BF16),
            dma((3, 2)),
            dma((3,)),
        ],
        info,
        half_0,
        half_1,
        *x_parts,
        z_here,
        z_after,
        z_before,
        in_specs=[SMEM] + [VMEM] * 2 + [HBM] * 8,
    )
    left = pltpu.VMEM((8, WIN, TWO), BF16)
    half_shape = shape(TWO, TWO)
    newest, x_newest, back_a, give_a = call(
        last_block,
        (half_shape, shape(VPAD, TWO), half_shape, half_shape),
        [left, dma((2,)), dma((2,))],
        info,
        half_0,
        half_1,
        *x_parts,
        z_far,
        early,
        wins_0,
        wins_1,
        in_specs=[SMEM] + [VMEM] * 2 + [HBM] * 5 + [VMEM] * 2 + [HBM] * 2,
    )
    got_a = across(give_a)
    back_b, give_b = call(
        second_half,
        (half_shape, half_shape),
        [left, dma((2,))],
        early,
        newest,
        x_newest,
        wins_0,
        wins_1,
        in_specs=[VMEM] * 3 + [HBM] * 2,
    )
    got_b = across(give_b)

    to_z = [None] + [(lambda dz: lambda z, x, c, y: (z + dz, x, c, y))(dz) for dz in range(1, 4)]
    to_x = lambda z, x, c, y: (z, x + 2, c, y)
    own_a, send_a = call(
        keep_x,
        (shape(4 * WIN, TWO, dtype=F32), shape(4 * WIN, TWO)),
        [left, dma((2,))],
        back_a,
        wins_0,
        wins_1,
        got_a,
        in_specs=[VMEM, HBM, HBM, VMEM],
    )
    from_x = move(send_a, to_x)
    own_b, *sends_b = call(
        keep_z,
        tuple([shape(2, WIN, TWO, dtype=F32)] + [shape(2, WIN, TWO)] * 3),
        [left, dma((2,))],
        back_b,
        wins_0,
        wins_1,
        got_b,
        in_specs=[VMEM, HBM, HBM, VMEM],
    )
    from_z = [move(send, to_z[dz]) for dz, send in enumerate(sends_b, start=1)]
    total_a, *sends_a = call(
        then_z, tuple([shape(WIN, TWO, dtype=F32)] + [shape(WIN, TWO)] * 3), [], own_a, from_x
    )
    last_z = [move(send, to_z[dz]) for dz, send in enumerate(sends_a, start=1)]
    total_a, from_z = lax.optimization_barrier((total_a, from_z))
    total_b, send_b = call(
        then_x, (shape(WIN, TWO, dtype=F32), shape(WIN, TWO)), [], own_b, *from_z
    )
    total_a = call(add_parts, shape(WIN, TWO, dtype=F32), [], total_a, *last_z, weight=10)
    share = VIRT * VIRT // 16
    first_row = grid_pos * BLK // 4
    first_cell = grid_pos * share - first_row * VIRT
    numbers = jnp.stack([pair_index[0], first_row, first_cell]).astype(jnp.int32)
    out = call(
        finish,
        shape(94, VIRT, dtype=F32),
        [pltpu.VMEM((WIN, VIRT), F32)],
        numbers,
        occ_energy.reshape(1, -1),
        vir_energy.reshape(1, -1),
        total_a,
        total_b,
        move(send_b, to_x),
        in_specs=[SMEM] + [VMEM] * 5,
    )
    return out.reshape(1, 94 * VIRT)[:, :share]


def solution(mesh):
    placed = (
        P("pair", None, None),
        P(None, "grid"),
        P("grid", "pair"),
        P("grid", "pair"),
        P("pair"),
        P(),
        P(),
    )
    return jax.shard_map(
        local, mesh=mesh, in_specs=placed, out_specs=P("pair", "grid"), check_vma=False
    )
```

profile of v0, /device:TPU:0, one launch (start us, length us, event | category | flops | bytes accessed | tf_op | source)
XLA Modules:
  0.0 121.7 jit_solution(3047118657325720955)
XLA Ops:
  0.0 0.0 collective-permute-start.2
  0.0 2.9 %shard_map.73.own_ref = bf16[384,768]{1,0:T(8,128)(2,1)} custom-call(bf16[375,750]{1,0:T(8,128)(2,1)} %z_hbm.1, f32[3,6]{1,0:T(4,128)} %s_ref.1), custom_call_target="tpu_custom_call" | custom-call | flops 1 | bytes 1 | tf_op jit(solution)/shard_map/pallas_call | solution.py:53
  2.9 1.7 %collective-permute-start = (bf16[384,768]{1,0:T(8,128)(2,1)}, bf16[384,768]{1,0:T(8,128)(2,1)}, u32[]{:S(2)}, u32[]{:S(2)}) collective-permute-start(bf16[384,768]{1,0:T(8,128)(2,1)} %shard_map.73.own_ref), channel_id=1, source_target_pairs={{0,1},{2,3},{4,5},{6,7},{8,9},{10,11},{12,13},{14,15},{1,17},{3,19... | collective-permute-start | bytes 1769480 | tf_op jit(solution)/shard_map/ppermute | solution.py:33
  4.6 1.5 %collective-permute-start.1 = (bf16[384,768]{1,0:T(8,128)(2,1)}, bf16[384,768]{1,0:T(8,128)(2,1)}, u32[]{:S(2)}, u32[]{:S(2)}) collective-permute-start(bf16[384,768]{1,0:T(8,128)(2,1)} %shard_map.73.own_ref), channel_id=1, source_target_pairs={{1,16},{3,18},{5,20},{7,22},{9,24},{11,26},{13,28},{15,30},{16,1},... | collective-permute-start | bytes 1769480 | tf_op jit(solution)/shard_map/ppermute | solution.py:33
  6.1 0.0 collective-permute-done.2.pair_ref
  6.1 1.9 %shard_map.74 = (bf16[2,1536,384]{2,1,0:T(8,128)(2,1)}, bf16[1536,384]{1,0:T(8,128)(2,1)S(1)}) custom-call(bf16[1500,375]{1,0:T(8,128)(2,1)S(1)} %copy-done.1, bf16[1500,375]{1,0:T(8,128)(2,1)S(1)} %collective-permute-done.2.pair_ref), custom_call_target="tpu_custom_call" | custom-call | flops 1 | bytes 1 | tf_op jit(solution)/shard_map/pallas_call | solution.py:53
  8.0 1.9 %collective-permute-start.6 = (bf16[2,1536,384]{2,1,0:T(8,128)(2,1)}, bf16[2,1536,384]{2,1,0:T(8,128)(2,1)S(1)}, u32[]{:S(2)}, u32[]{:S(2)}) collective-permute-start(bf16[2,1536,384]{2,1,0:T(8,128)(2,1)} %get-tuple-element.54.refs_0_), channel_id=1, source_target_pairs={{0,32},{2,34},{4,36},{6,38},{8,104},{10,106},{12,108},{14,110},{1,... | collective-permute-start | bytes 7077896 | tf_op jit(solution)/shard_map/ppermute | solution.py:33
  9.9 0.1 stack.80.info
  10.0 0.0 copy-start
  10.0 2.3 %copy-done = bf16[1,1500,1500]{2,1,0:T(8,128)(2,1)S(1)} copy-done((bf16[1,1500,1500]{2,1,0:T(8,128)(2,1)S(1)}, bf16[1,1500,1500]{2,1,0:T(8,128)(2,1)}, u32[]{:S(2)}) %copy-start) | copy-done | bytes 4500024
  12.3 2.8 %shard_map.75 = (bf16[384,1536]{1,0:T(8,128)(2,1)S(1)}, bf16[2,8,96,384]{3,2,1,0:T(8,128)(2,1)S(1)}) custom-call(s32[16]{0:T(128)S(1)} %stack.80.info, bf16[1536,384]{1,0:T(8,128)(2,1)S(1)} %get-tuple-element.53.x_ref, bf16[1,1500,1500]{2,1,0:T(8,128)(2,1)S(1)} %copy-done), custom_call_target="tpu_custom_call" | custom-call | flops 1 | bytes 1 | tf_op jit(solution)/shard_map/pallas_call | solution.py:53
  15.1 5.3 %collective-permute-done.a_ref = bf16[384,768]{1,0:T(8,128)(2,1)} collective-permute-done((bf16[384,768]{1,0:T(8,128)(2,1)}, bf16[384,768]{1,0:T(8,128)(2,1)}, u32[]{:S(2)}, u32[]{:S(2)}) %collective-permute-start) | collective-permute-done | bytes 589856 | tf_op jit(solution)/shard_map/ppermute | solution.py:33
  20.4 0.0 collective-permute-done.1.b_ref
  20.4 2.9 %collective-permute-start.5 = (bf16[1536,384]{1,0:T(8,128)(2,1)S(1)}, bf16[1536,384]{1,0:T(8,128)(2,1)S(1)}, u32[]{:S(2)}, u32[]{:S(2)}) collective-permute-start(bf16[1536,384]{1,0:T(8,128)(2,1)S(1)} %get-tuple-element.53.x_ref), channel_id=1, source_target_pairs={{0,17},{2,19},{4,21},{6,23},{8,25},{10,27},{12,29},{14,31},{1,16},... | collective-permute-start | bytes 3538952 | tf_op jit(solution)/shard_map/ppermute | solution.py:33
  23.4 1.3 %shard_map.76.refs_5_ = bf16[2,384,768]{2,1,0:T(8,128)(2,1)S(1)} custom-call(s32[16]{0:T(128)S(1)} %stack.80.info, bf16[384,768]{1,0:T(8,128)(2,1)S(1)} %copy-done.2, bf16[384,768]{1,0:T(8,128)(2,1)} %collective-permute-done.a_ref, bf16[384,768]{1,0:T(8,128)(2,1)} %collective-permute-done.1.b_ref), custom_call_target="tpu_custom_call" | custom-call | flops 20000000000 | bytes 20000000 | tf_op jit(solution)/shard_map/pallas_call | solution.py:53
  24.7 1.6 %collective-permute-start.3 = (bf16[2,384,768]{2,1,0:T(8,128)(2,1)S(1)}, bf16[2,384,768]{2,1,0:T(8,128)(2,1)S(1)}, u32[]{:S(2)}, u32[]{:S(2)}) collective-permute-start(bf16[2,384,768]{2,1,0:T(8,128)(2,1)S(1)} %shard_map.76.refs_5_), channel_id=1, source_target_pairs={{0,2},{2,4},{4,6},{6,0},{8,10},{10,12},{12,14},{14,8},{1,3},{3,5},... | collective-permute-start | bytes 3538952 | tf_op jit(solution)/shard_map/ppermute | solution.py:33
  26.4 1.7 %collective-permute-start.4 = (bf16[2,384,768]{2,1,0:T(8,128)(2,1)S(1)}, bf16[2,384,768]{2,1,0:T(8,128)(2,1)S(1)}, u32[]{:S(2)}, u32[]{:S(2)}) collective-permute-start(bf16[2,384,768]{2,1,0:T(8,128)(2,1)S(1)} %shard_map.76.refs_5_), channel_id=1, source_target_pairs={{0,6},{2,0},{4,2},{6,4},{8,14},{10,8},{12,10},{14,12},{1,7},{3,1},... | collective-permute-start | bytes 3538952 | tf_op jit(solution)/shard_map/ppermute | solution.py:33
  28.0 11.0 %collective-permute-done.6.refs_1_ = bf16[2,1536,384]{2,1,0:T(8,128)(2,1)S(1)} collective-permute-done((bf16[2,1536,384]{2,1,0:T(8,128)(2,1)}, bf16[2,1536,384]{2,1,0:T(8,128)(2,1)S(1)}, u32[]{:S(2)}, u32[]{:S(2)}) %collective-permute-start.6) | collective-permute-done | bytes 2359328 | tf_op jit(solution)/shard_map/ppermute | solution.py:33
  39.0 0.1 slice_bitcast_fusion
  39.2 0.1 collective-permute-start.8
  39.2 2.2 %collective-permute-start.7 = (bf16[2,1536,384]{2,1,0:T(8,128)(2,1)S(1)}, bf16[2,1536,384]{2,1,0:T(8,128)(2,1)S(1)}, u32[]{:S(2)}, u32[]{:S(2)}) collective-permute-start(bf16[2,1536,384]{2,1,0:T(8,128)(2,1)S(1)} %collective-permute-done.6.refs_1_), channel_id=1, source_target_pairs={{0,8},{2,10},{4,12},{6,14},{8,0},{10,2},{12,4},{14,6},{1,9},{3,11}... | collective-permute-start | bytes 7077896 | tf_op jit(solution)/shard_map/ppermute | solution.py:33
  41.4 0.3 shard_map.77.amp_ref
  41.7 7.5 %collective-permute-done.5.x_ref = bf16[1536,384]{1,0:T(8,128)(2,1)S(1)} collective-permute-done((bf16[1536,384]{1,0:T(8,128)(2,1)S(1)}, bf16[1536,384]{1,0:T(8,128)(2,1)S(1)}, u32[]{:S(2)}, u32[]{:S(2)}) %collective-permute-start.5) | collective-permute-done | bytes 1179680 | tf_op jit(solution)/shard_map/ppermute | solution.py:33
  49.2 2.8 %shard_map.78 = (bf16[384,1536]{1,0:T(8,128)(2,1)S(1)}, bf16[2,8,96,384]{3,2,1,0:T(8,128)(2,1)S(1)}) custom-call(s32[16]{0:T(128)S(1)} %stack.80.info, bf16[1536,384]{1,0:T(8,128)(2,1)S(1)} %collective-permute-done.5.x_ref, bf16[1,1500,1500]{2,1,0:T(8,128)(2,1)S(1)} %shard_map.77.amp_ref), custom_call_target="tpu_custom_call" | custom-call | flops 10000000000 | bytes 10000001 | tf_op jit(solution)/shard_map/pallas_call | solution.py:53
  52.0 1.2 %collective-permute-done.3.first_ref.refs_7_ = bf16[2,384,768]{2,1,0:T(8,128)(2,1)S(1)} collective-permute-done((bf16[2,384,768]{2,1,0:T(8,128)(2,1)S(1)}, bf16[2,384,768]{2,1,0:T(8,128)(2,1)S(1)}, u32[]{:S(2)}, u32[]{:S(2)}) %collective-permute-start.3) | collective-permute-done | bytes 1179680 | tf_op jit(solution)/shard_map/ppermute | solution.py:33
  53.2 0.0 collective-permute-done.4.second_ref.refs_6_
  53.2 0.6 shard_map.79
  53.9 2.8 %collective-permute-done.8.refs_3_ = bf16[1536,384]{1,0:T(8,128)(2,1)S(1)} collective-permute-done((bf16[1536,384]{1,0:T(8,128)(2,1)S(1)}, bf16[1536,384]{1,0:T(8,128)(2,1)S(1)}, u32[]{:S(2)}, u32[]{:S(2)}) %collective-permute-start.8) | collective-permute-done | bytes 1179680 | tf_op jit(solution)/shard_map/ppermute | solution.py:33
  56.6 0.0 collective-permute-start.9
  56.6 1.6 %collective-permute-start.10 = (bf16[2,384,768]{2,1,0:T(8,128)(2,1)S(1)}, bf16[2,384,768]{2,1,0:T(8,128)(2,1)S(1)}, u32[]{:S(2)}, u32[]{:S(2)}) collective-permute-start(bf16[2,384,768]{2,1,0:T(8,128)(2,1)S(1)} %shard_map.79), channel_id=1, source_target_pairs={{0,2},{2,4},{4,6},{6,0},{8,14},{10,8},{12,10},{14,12},{1,3},{3,5},... | collective-permute-start | bytes 3538952 | tf_op jit(solution)/shard_map/ppermute | solution.py:33
  58.2 1.3 %collective-permute-done.9.refs_4_ = bf16[1536,384]{1,0:T(8,128)(2,1)S(1)} collective-permute-done((bf16[1536,384]{1,0:T(8,128)(2,1)S(1)}, bf16[1536,384]{1,0:T(8,128)(2,1)S(1)}, u32[]{:S(2)}, u32[]{:S(2)}) %collective-permute-start.9) | collective-permute-done | bytes 1179680 | tf_op jit(solution)/shard_map/ppermute | solution.py:33
  59.5 0.0 collective-permute-done.7.refs_2_
  59.5 15.3 %shard_map.80.refs_6_.early_ref = f32[768,1536]{1,0:T(8,128)S(1)} custom-call(s32[16]{0:T(128)S(1)} %stack.80.info, bf16[384,1536]{1,0:T(8,128)(2,1)S(1)} %get-tuple-element.49.h0_ref, bf16[384,1536]{1,0:T(8,128)(2,1)S(1)} %get-tuple-element.59.h1_ref, bf16[2,1536,384]{2,1,0:T(8,128)(2,1)} %get-tuple-element.54.refs_0_, ...), custom_call_target="tpu_custom_call" | custom-call | flops 1 | bytes 1 | tf_op jit(solution)/shard_map/pallas_call | solution.py:53
  74.8 5.6 %shard_map.81 = (bf16[768,768]{1,0:T(8,128)(2,1)S(1)}, bf16[1536,768]{1,0:T(8,128)(2,1)S(1)}, bf16[768,768]{1,0:T(8,128)(2,1)S(1)}, bf16[768,768]{1,0:T(8,128)(2,1)S(1)}) custom-call(s32[16]{0:T(128)S(1)} %stack.80.info, bf16[384,1536]{1,0:T(8,128)(2,1)S(1)} %get-tuple-element.49.h0_ref, bf16[384,1536]{1,0:T(8,128)(2,1)S(1)} %get-tuple-element.59.h1_ref, ...), custom_call_target="tpu_custom_call" | custom-call | flops 1 | bytes 1 | tf_op jit(solution)/shard_map/pallas_call | solution.py:53
  80.4 0.5 collective-permute-start.11
  80.8 2.9 %shard_map.84 = (bf16[768,768]{1,0:T(8,128)(2,1)S(1)}, bf16[768,768]{1,0:T(8,128)(2,1)S(1)}) custom-call(f32[768,1536]{1,0:T(8,128)S(1)} %shard_map.80.refs_6_.early_ref, bf16[768,768]{1,0:T(8,128)(2,1)S(1)} %get-tuple-element.70.newest_ref, bf16[1536,768]{1,0:T(8,128)(2,1)S(1)} %get-tuple-element.71.xn_ref, ...), custom_call_target="tpu_custom_call" | custom-call | flops 1 | bytes 1 | tf_op jit(solution)/shard_map/pallas_call | solution.py:53
  83.8 0.4 collective-permute-start.13
  84.2 1.2 %shard_map.82 = (f32[384,768]{1,0:T(8,128)S(1)}, bf16[384,768]{1,0:T(8,128)(2,1)S(1)}) custom-call(bf16[768,768]{1,0:T(8,128)(2,1)S(1)} %get-tuple-element.65.back_ref, bf16[2,8,96,384]{3,2,1,0:T(8,128)(2,1)S(1)} %get-tuple-element.63.refs_7_.w0_ref, bf16[2,8,96,384]{3,2,1,0:T(8,128)(2,1)S(1)} %get-tuple-element.64.refs_8_.w1_ref, ...), custom_call_target="tpu_custom_call" | custom-call | flops 1 | bytes 1 | tf_op jit(solution)/shard_map/pallas_call | solution.py:53
  85.4 4.7 %collective-permute-start.12 = (bf16[384,768]{1,0:T(8,128)(2,1)S(1)}, bf16[384,768]{1,0:T(8,128)(2,1)S(1)}, u32[]{:S(2)}, u32[]{:S(2)}) collective-permute-start(bf16[384,768]{1,0:T(8,128)(2,1)S(1)} %get-tuple-element.68), channel_id=1, source_target_pairs={{0,16},{2,18},{4,20},{6,22},{8,24},{10,26},{12,28},{14,30},{1,17},... | collective-permute-start | bytes 1769480 | tf_op jit(solution)/shard_map/ppermute | solution.py:33
  90.1 2.1 %shard_map.85 = (f32[2,96,768]{2,1,0:T(8,128)S(1)}, bf16[2,96,768]{2,1,0:T(8,128)(2,1)S(1)}, bf16[2,96,768]{2,1,0:T(8,128)(2,1)}, bf16[2,96,768]{2,1,0:T(8,128)(2,1)}) custom-call(bf16[768,768]{1,0:T(8,128)(2,1)S(1)} %get-tuple-element.72.back_ref, bf16[2,8,96,384]{3,2,1,0:T(8,128)(2,1)S(1)} %get-tuple-element.63.refs_7_.w0_ref, ...), custom_call_target="tpu_custom_call" | custom-call | flops 1 | bytes 1 | tf_op jit(solution)/shard_map/pallas_call | solution.py:53
  92.2 0.8 copy-done.3
  93.0 0.0 collective-permute-start.14
  93.0 2.3 %collective-permute-start.15 = (bf16[2,96,768]{2,1,0:T(8,128)(2,1)}, bf16[2,96,768]{2,1,0:T(8,128)(2,1)}, u32[]{:S(2)}, u32[]{:S(2)}) collective-permute-start(bf16[2,96,768]{2,1,0:T(8,128)(2,1)} %get-tuple-element.75), channel_id=1, source_target_pairs={{0,64},{2,66},{4,68},{6,70},{8,72},{10,74},{12,76},{14,78},{1,65},... | collective-permute-start | bytes 884744 | tf_op jit(solution)/shard_map/ppermute | solution.py:33
  95.3 2.5 %collective-permute-start.16 = (bf16[2,96,768]{2,1,0:T(8,128)(2,1)}, bf16[2,96,768]{2,1,0:T(8,128)(2,1)}, u32[]{:S(2)}, u32[]{:S(2)}) collective-permute-start(bf16[2,96,768]{2,1,0:T(8,128)(2,1)} %get-tuple-element.76), channel_id=1, source_target_pairs={{0,96},{2,98},{4,100},{6,102},{8,104},{10,106},{12,108},{14,110},{... | collective-permute-start | bytes 884744 | tf_op jit(solution)/shard_map/ppermute | solution.py:33
  97.8 6.3 %collective-permute-done.12.got_ref = bf16[384,768]{1,0:T(8,128)(2,1)S(1)} collective-permute-done((bf16[384,768]{1,0:T(8,128)(2,1)S(1)}, bf16[384,768]{1,0:T(8,128)(2,1)S(1)}, u32[]{:S(2)}, u32[]{:S(2)}) %collective-permute-start.12) | collective-permute-done | bytes 589856 | tf_op jit(solution)/shard_map/ppermute | solution.py:33
  104.0 0.8 shard_map.83
  104.8 0.7 copy-done.6
  105.5 2.3 %collective-permute-start.18 = (bf16[96,768]{1,0:T(8,128)(2,1)}, bf16[96,768]{1,0:T(8,128)(2,1)S(1)}, u32[]{:S(2)}, u32[]{:S(2)}) collective-permute-start(bf16[96,768]{1,0:T(8,128)(2,1)} %get-tuple-element.79), channel_id=1, source_target_pairs={{0,64},{2,66},{4,68},{6,70},{8,72},{10,74},{12,76},{14,78},{1,65},... | collective-permute-start | bytes 442376 | tf_op jit(solution)/shard_map/ppermute | solution.py:33
  107.8 1.9 %collective-permute-done.14.got_1 = bf16[2,96,768]{2,1,0:T(8,128)(2,1)S(1)} collective-permute-done((bf16[2,96,768]{2,1,0:T(8,128)(2,1)S(1)}, bf16[2,96,768]{2,1,0:T(8,128)(2,1)S(1)}, u32[]{:S(2)}, u32[]{:S(2)}) %collective-permute-start.14) | collective-permute-done | bytes 294944 | tf_op jit(solution)/shard_map/ppermute | solution.py:33
  109.7 0.6 collective-permute-start.19
  111.0 0.1 pad_add_fusion.numbers
  111.0 0.0 collective-permute-done.15.got_2
  111.0 0.0 collective-permute-done.16.got_3
  111.0 1.2 shard_map.87
  112.2 0.0 copy-start.5
  112.2 3.4 %collective-permute-start.20 = (bf16[96,768]{1,0:T(8,128)(2,1)S(1)}, bf16[96,768]{1,0:T(8,128)(2,1)S(1)}, u32[]{:S(2)}, u32[]{:S(2)}) collective-permute-start(bf16[96,768]{1,0:T(8,128)(2,1)S(1)} %get-tuple-element.86), channel_id=1, source_target_pairs={{0,16},{2,18},{4,20},{6,22},{8,24},{10,26},{12,28},{14,30},{1,17},... | collective-permute-start | bytes 442376 | tf_op jit(solution)/shard_map/ppermute | solution.py:33
  115.6 0.4 collective-permute-done.17.refs_0_
  115.9 0.0 collective-permute-done.18.refs_1_
  115.9 0.9 collective-permute-done.19.refs_2_
  116.8 0.1 shard_map.86.a_ref
  116.9 2.1 %collective-permute-done.20.b1_ref = bf16[96,768]{1,0:T(8,128)(2,1)S(1)} collective-permute-done((bf16[96,768]{1,0:T(8,128)(2,1)S(1)}, bf16[96,768]{1,0:T(8,128)(2,1)S(1)}, u32[]{:S(2)}, u32[]{:S(2)}) %collective-permute-start.20) | collective-permute-done | bytes 147488 | tf_op jit(solution)/shard_map/ppermute | solution.py:33
  119.0 0.9 shard_map.88
  119.9 0.9 reshape.11
  120.8 0.8 slice.9
  (23 shorter events, 0.0 us)
Async XLA Ops:
  0.0 6.1 %copy-start.1 = (bf16[1500,375]{1,0:T(8,128)(2,1)S(1)}, bf16[1500,375]{1,0:T(8,128)(2,1)}, u32[]{:S(2)}) copy-start(bf16[1500,375]{1,0:T(8,128)(2,1)} %own_ref.1) | copy-start | bytes 3375004
  0.0 6.1 %collective-permute-start.2 = (bf16[1500,375]{1,0:T(8,128)(2,1)}, bf16[1500,375]{1,0:T(8,128)(2,1)S(1)}, u32[]{:S(2)}, u32[]{:S(2)}) collective-permute-start(bf16[1500,375]{1,0:T(8,128)(2,1)} %own_ref.1), channel_id=1, source_target_pairs={{0,8},{2,10},{4,12},{6,14},{8,0},{10,2},{12,4},{14,6},{1,9},{3,11}... | collective-permute-start | bytes 3375008 | tf_op jit(solution)/shard_map/ppermute | solution.py:33
  2.9 17.5 %collective-permute-start = (bf16[384,768]{1,0:T(8,128)(2,1)}, bf16[384,768]{1,0:T(8,128)(2,1)}, u32[]{:S(2)}, u32[]{:S(2)}) collective-permute-start(bf16[384,768]{1,0:T(8,128)(2,1)} %shard_map.73.own_ref), channel_id=1, source_target_pairs={{0,1},{2,3},{4,5},{6,7},{8,9},{10,11},{12,13},{14,15},{1,17},{3,19... | collective-permute-start | bytes 1769480 | tf_op jit(solution)/shard_map/ppermute | solution.py:33
  4.6 15.8 %collective-permute-start.1 = (bf16[384,768]{1,0:T(8,128)(2,1)}, bf16[384,768]{1,0:T(8,128)(2,1)}, u32[]{:S(2)}, u32[]{:S(2)}) collective-permute-start(bf16[384,768]{1,0:T(8,128)(2,1)} %shard_map.73.own_ref), channel_id=1, source_target_pairs={{1,16},{3,18},{5,20},{7,22},{9,24},{11,26},{13,28},{15,30},{16,1},... | collective-permute-start | bytes 1769480 | tf_op jit(solution)/shard_map/ppermute | solution.py:33
  8.0 31.1 %collective-permute-start.6 = (bf16[2,1536,384]{2,1,0:T(8,128)(2,1)}, bf16[2,1536,384]{2,1,0:T(8,128)(2,1)S(1)}, u32[]{:S(2)}, u32[]{:S(2)}) collective-permute-start(bf16[2,1536,384]{2,1,0:T(8,128)(2,1)} %get-tuple-element.54.refs_0_), channel_id=1, source_target_pairs={{0,32},{2,34},{4,36},{6,38},{8,104},{10,106},{12,108},{14,110},{1,... | collective-permute-start | bytes 7077896 | tf_op jit(solution)/shard_map/ppermute | solution.py:33
  10.0 2.3 %copy-start = (bf16[1,1500,1500]{2,1,0:T(8,128)(2,1)S(1)}, bf16[1,1500,1500]{2,1,0:T(8,128)(2,1)}, u32[]{:S(2)}) copy-start(bf16[1,1500,1500]{2,1,0:T(8,128)(2,1)} %in_ref) | copy-start | bytes 13500004
  12.3 11.1 %copy-start.2 = (bf16[384,768]{1,0:T(8,128)(2,1)S(1)}, bf16[384,768]{1,0:T(8,128)(2,1)}, u32[]{:S(2)}) copy-start(bf16[384,768]{1,0:T(8,128)(2,1)} %shard_map.73.own_ref) | copy-start | bytes 1769476
  20.4 21.0 %slice-start = ((s8[4620288]{0:T(1024)(128)(4,1)}), s8[4194304]{0:T(1024)(128)(4,1)S(1)}, s32[]{:S(2)}) async-start(s8[4620288]{0:T(1024)(128)(4,1)} %bitcast.20), calls=%async_computation | async-start | bytes 8388608
  20.4 21.0 %slice-start.1 = ((s8[4620288]{0:T(1024)(128)(4,1)}), s8[425984]{0:T(1024)(128)(4,1)S(1)}, s32[]{:S(2)}) async-start(s8[4620288]{0:T(1024)(128)(4,1)} %bitcast.20), calls=%async_computation.1 | async-start | bytes 851968
  20.4 28.7 %collective-permute-start.5 = (bf16[1536,384]{1,0:T(8,128)(2,1)S(1)}, bf16[1536,384]{1,0:T(8,128)(2,1)S(1)}, u32[]{:S(2)}, u32[]{:S(2)}) collective-permute-start(bf16[1536,384]{1,0:T(8,128)(2,1)S(1)} %get-tuple-element.53.x_ref), channel_id=1, source_target_pairs={{0,17},{2,19},{4,21},{6,23},{8,25},{10,27},{12,29},{14,31},{1,16},... | collective-permute-start | bytes 3538952 | tf_op jit(solution)/shard_map/ppermute | solution.py:33
  24.7 28.5 %collective-permute-start.3 = (bf16[2,384,768]{2,1,0:T(8,128)(2,1)S(1)}, bf16[2,384,768]{2,1,0:T(8,128)(2,1)S(1)}, u32[]{:S(2)}, u32[]{:S(2)}) collective-permute-start(bf16[2,384,768]{2,1,0:T(8,128)(2,1)S(1)} %shard_map.76.refs_5_), channel_id=1, source_target_pairs={{0,2},{2,4},{4,6},{6,0},{8,10},{10,12},{12,14},{14,8},{1,3},{3,5},... | collective-permute-start | bytes 3538952 | tf_op jit(solution)/shard_map/ppermute | solution.py:33
  26.4 26.9 %collective-permute-start.4 = (bf16[2,384,768]{2,1,0:T(8,128)(2,1)S(1)}, bf16[2,384,768]{2,1,0:T(8,128)(2,1)S(1)}, u32[]{:S(2)}, u32[]{:S(2)}) collective-permute-start(bf16[2,384,768]{2,1,0:T(8,128)(2,1)S(1)} %shard_map.76.refs_5_), channel_id=1, source_target_pairs={{0,6},{2,0},{4,2},{6,4},{8,14},{10,8},{12,10},{14,12},{1,7},{3,1},... | collective-permute-start | bytes 3538952 | tf_op jit(solution)/shard_map/ppermute | solution.py:33
  39.2 17.5 %collective-permute-start.8 = (bf16[1536,384]{1,0:T(8,128)(2,1)S(1)}, bf16[1536,384]{1,0:T(8,128)(2,1)S(1)}, u32[]{:S(2)}, u32[]{:S(2)}) collective-permute-start(bf16[1536,384]{1,0:T(8,128)(2,1)S(1)} %slice_bitcast_fusion), channel_id=1, source_target_pairs={{0,32},{2,34},{4,36},{6,38},{8,104},{10,106},{12,108},{14,110},{1,... | collective-permute-start | bytes 3538952 | tf_op jit(solution)/shard_map/ppermute | solution.py:33
  39.2 20.3 %collective-permute-start.7 = (bf16[2,1536,384]{2,1,0:T(8,128)(2,1)S(1)}, bf16[2,1536,384]{2,1,0:T(8,128)(2,1)S(1)}, u32[]{:S(2)}, u32[]{:S(2)}) collective-permute-start(bf16[2,1536,384]{2,1,0:T(8,128)(2,1)S(1)} %collective-permute-done.6.refs_1_), channel_id=1, source_target_pairs={{0,8},{2,10},{4,12},{6,14},{8,0},{10,2},{12,4},{14,6},{1,9},{3,11}... | collective-permute-start | bytes 7077896 | tf_op jit(solution)/shard_map/ppermute | solution.py:33
  56.6 2.8 %collective-permute-start.9 = (bf16[1536,384]{1,0:T(8,128)(2,1)S(1)}, bf16[1536,384]{1,0:T(8,128)(2,1)S(1)}, u32[]{:S(2)}, u32[]{:S(2)}) collective-permute-start(bf16[1536,384]{1,0:T(8,128)(2,1)S(1)} %collective-permute-done.8.refs_3_), channel_id=1, source_target_pairs={{0,8},{2,10},{4,12},{6,14},{8,0},{10,2},{12,4},{14,6},{1,9},{3,11}... | collective-permute-start | bytes 3538952 | tf_op jit(solution)/shard_map/ppermute | solution.py:33
  56.6 18.1 %collective-permute-start.10 = (bf16[2,384,768]{2,1,0:T(8,128)(2,1)S(1)}, bf16[2,384,768]{2,1,0:T(8,128)(2,1)S(1)}, u32[]{:S(2)}, u32[]{:S(2)}) collective-permute-start(bf16[2,384,768]{2,1,0:T(8,128)(2,1)S(1)} %shard_map.79), channel_id=1, source_target_pairs={{0,2},{2,4},{4,6},{6,0},{8,14},{10,8},{12,10},{14,12},{1,3},{3,5},... | collective-permute-start | bytes 3538952 | tf_op jit(solution)/shard_map/ppermute | solution.py:33
  80.4 3.8 %collective-permute-start.11 = (bf16[768,768]{1,0:T(8,128)(2,1)S(1)}, bf16[768,768]{1,0:T(8,128)(2,1)S(1)}, u32[]{:S(2)}, u32[]{:S(2)}) collective-permute-start(bf16[768,768]{1,0:T(8,128)(2,1)S(1)} %get-tuple-element.66), channel_id=1, source_target_pairs={{0,8},{2,10},{4,12},{6,14},{8,0},{10,2},{12,4},{14,6},{1,9},{3,11}... | collective-permute-start | bytes 3538952 | tf_op jit(solution)/shard_map/ppermute | solution.py:33
  83.8 6.4 %collective-permute-start.13 = (bf16[768,768]{1,0:T(8,128)(2,1)S(1)}, bf16[768,768]{1,0:T(8,128)(2,1)S(1)}, u32[]{:S(2)}, u32[]{:S(2)}) collective-permute-start(bf16[768,768]{1,0:T(8,128)(2,1)S(1)} %get-tuple-element.73), channel_id=1, source_target_pairs={{0,8},{2,10},{4,12},{6,14},{8,0},{10,2},{12,4},{14,6},{1,9},{3,11}... | collective-permute-start | bytes 3538952 | tf_op jit(solution)/shard_map/ppermute | solution.py:33
  85.4 18.6 %collective-permute-start.12 = (bf16[384,768]{1,0:T(8,128)(2,1)S(1)}, bf16[384,768]{1,0:T(8,128)(2,1)S(1)}, u32[]{:S(2)}, u32[]{:S(2)}) collective-permute-start(bf16[384,768]{1,0:T(8,128)(2,1)S(1)} %get-tuple-element.68), channel_id=1, source_target_pairs={{0,16},{2,18},{4,20},{6,22},{8,24},{10,26},{12,28},{14,30},{1,17},... | collective-permute-start | bytes 1769480 | tf_op jit(solution)/shard_map/ppermute | solution.py:33
  92.2 0.8 copy-start.3
  93.0 17.9 %copy-start.8 = (f32[1500]{0:T(1024)S(1)}, f32[1500]{0:T(1024)}, u32[]{:S(2)}) copy-start(f32[1500]{0:T(1024)} %param.12) | copy-start | bytes 18004
  93.0 18.0 %copy-start.4 = (f32[2,96,768]{2,1,0:T(8,128)S(1)}, f32[2,96,768]{2,1,0:T(8,128)}, u32[]{:S(2)}) copy-start(f32[2,96,768]{2,1,0:T(8,128)} %copy-done.3) | copy-start | bytes 1769476
  93.0 16.7 %collective-permute-start.14 = (bf16[2,96,768]{2,1,0:T(8,128)(2,1)S(1)}, bf16[2,96,768]{2,1,0:T(8,128)(2,1)S(1)}, u32[]{:S(2)}, u32[]{:S(2)}) collective-permute-start(bf16[2,96,768]{2,1,0:T(8,128)(2,1)S(1)} %get-tuple-element.74), channel_id=1, source_target_pairs={{0,32},{2,34},{4,36},{6,38},{8,40},{10,42},{12,44},{14,46},{1,33},... | collective-permute-start | bytes 884744 | tf_op jit(solution)/shard_map/ppermute | solution.py:33
  93.0 18.0 %collective-permute-start.15 = (bf16[2,96,768]{2,1,0:T(8,128)(2,1)}, bf16[2,96,768]{2,1,0:T(8,128)(2,1)}, u32[]{:S(2)}, u32[]{:S(2)}) collective-permute-start(bf16[2,96,768]{2,1,0:T(8,128)(2,1)} %get-tuple-element.75), channel_id=1, source_target_pairs={{0,64},{2,66},{4,68},{6,70},{8,72},{10,74},{12,76},{14,78},{1,65},... | collective-permute-start | bytes 884744 | tf_op jit(solution)/shard_map/ppermute | solution.py:33
  95.3 15.7 %collective-permute-start.16 = (bf16[2,96,768]{2,1,0:T(8,128)(2,1)}, bf16[2,96,768]{2,1,0:T(8,128)(2,1)}, u32[]{:S(2)}, u32[]{:S(2)}) collective-permute-start(bf16[2,96,768]{2,1,0:T(8,128)(2,1)} %get-tuple-element.76), channel_id=1, source_target_pairs={{0,96},{2,98},{4,100},{6,102},{8,104},{10,106},{12,108},{14,110},{... | collective-permute-start | bytes 884744 | tf_op jit(solution)/shard_map/ppermute | solution.py:33
  104.8 0.7 copy-start.6
  105.5 11.3 %copy-start.7 = (f32[96,768]{1,0:T(8,128)S(1)}, f32[96,768]{1,0:T(8,128)}, u32[]{:S(2)}) copy-start(f32[96,768]{1,0:T(8,128)} %copy-done.6) | copy-start | bytes 884740
  105.5 10.4 %collective-permute-start.17 = (bf16[96,768]{1,0:T(8,128)(2,1)}, bf16[96,768]{1,0:T(8,128)(2,1)S(1)}, u32[]{:S(2)}, u32[]{:S(2)}) collective-permute-start(bf16[96,768]{1,0:T(8,128)(2,1)} %get-tuple-element.78), channel_id=1, source_target_pairs={{0,32},{2,34},{4,36},{6,38},{8,40},{10,42},{12,44},{14,46},{1,33},... | collective-permute-start | bytes 442376 | tf_op jit(solution)/shard_map/ppermute | solution.py:33
  105.5 10.4 %collective-permute-start.18 = (bf16[96,768]{1,0:T(8,128)(2,1)}, bf16[96,768]{1,0:T(8,128)(2,1)S(1)}, u32[]{:S(2)}, u32[]{:S(2)}) collective-permute-start(bf16[96,768]{1,0:T(8,128)(2,1)} %get-tuple-element.79), channel_id=1, source_target_pairs={{0,64},{2,66},{4,68},{6,70},{8,72},{10,74},{12,76},{14,78},{1,65},... | collective-permute-start | bytes 442376 | tf_op jit(solution)/shard_map/ppermute | solution.py:33
  109.7 7.1 %collective-permute-start.19 = (bf16[96,768]{1,0:T(8,128)(2,1)S(1)}, bf16[96,768]{1,0:T(8,128)(2,1)S(1)}, u32[]{:S(2)}, u32[]{:S(2)}) collective-permute-start(bf16[96,768]{1,0:T(8,128)(2,1)S(1)} %get-tuple-element.80), channel_id=1, source_target_pairs={{0,96},{2,98},{4,100},{6,102},{8,104},{10,106},{12,108},{14,110},{... | collective-permute-start | bytes 442376 | tf_op jit(solution)/shard_map/ppermute | solution.py:33
  112.2 6.7 %copy-start.5 = (f32[150]{0:T(256)S(1)}, f32[150]{0:T(256)}, u32[]{:S(2)}) copy-start(f32[150]{0:T(256)} %param.13) | copy-start | bytes 1804
  112.2 6.7 %collective-permute-start.20 = (bf16[96,768]{1,0:T(8,128)(2,1)S(1)}, bf16[96,768]{1,0:T(8,128)(2,1)S(1)}, u32[]{:S(2)}, u32[]{:S(2)}) collective-permute-start(bf16[96,768]{1,0:T(8,128)(2,1)S(1)} %get-tuple-element.86), channel_id=1, source_target_pairs={{0,16},{2,18},{4,20},{6,22},{8,24},{10,26},{12,28},{14,30},{1,17},... | collective-permute-start | bytes 442376 | tf_op jit(solution)/shard_map/ppermute | solution.py:33
where the time goes:
time: 123 us; the launch traced here: 122 us
  Pallas kernels  42.6 us (35%)
  waiting for transfers between devices  40.6 us (33%)
  starting transfers between devices  31.6 us (26%)
  local copies, waits for them, and re-layouts  5.89 us (5%)
    pallas_call x16, Pallas kernels, call(): pl.pallas_call(kernel, out_shape=out_shape, in_specs=in_specs or [VMEM] *...  42.6 us
    ppermute x21, waiting for transfers between devices, move(): return lax.ppermute(block, BOTH, pairs)  40.6 us
    ppermute x21, starting transfers between devices, move(): return lax.ppermute(block, BOTH, pairs)  31.6 us
    unnamed x22, local copies, waits for them, and re-layouts  3.87 us
  transfers between devices with their start and end apart: 21, of which 11 were waited for; matrix products, arithmetic and copies ran while one was open for 0% of the time, Pallas kernels for 30%

commit v1 on v0

--- a/solution.py
+++ b/solution.py
@@ -48,7 +48,7 @@
 HBM = pl.BlockSpec(memory_space=pl.ANY)
 
 
-def call(kernel, out_shape, scratch, *args, in_specs=None, out_specs=None, mib=20, weight=0):
+def call(kernel, out_shape, scratch, *args, in_specs=None, out_specs=None, mib=12, weight=0):
     many = isinstance(out_shape, (tuple, list))
     return pl.pallas_call(
         kernel,
@@ -61,14 +61,10 @@
     )(*args)
 
 
-def pad_metric(z_hbm, s_ref, z_out, tmp, z_ref, sem):
+def pad_metric(z_hbm, s_ref, z_out, tail, z_ref, sem):
     load = pltpu.make_async_copy(z_hbm, z_ref, sem)
     load.start()
-    tmp[...] = jnp.zeros_like(tmp)
-    load.wait()
-    z = z_ref[...].astype(F32)
-    tmp[:BLK, :BLK] = z[:, :BLK]
-    tmp[:BLK, BPAD : BPAD + BLK] = z[:, BLK:]
+    tail[...] = jnp.zeros_like(tail)
     lane = lax.broadcasted_iota(jnp.int32, (1, TWO), 1)
     for r in range(3):
         row = jnp.zeros((1, TWO), F32)
@@ -77,17 +73,23 @@
             row = jnp.where((lane >= start) & (lane < start + ZBLK), s_ref[r, q], row)
         for part in range(3):
             piece = row.astype(BF16).astype(F32)
-            tmp[BLK + 3 * part + r : BLK + 3 * part + r + 1, :] = piece
+            tail[7 + 3 * part + r : 8 + 3 * part + r, :] = piece
             row = row - piece
-    z_out[...] = tmp[...].astype(BF16)
+    load.wait()
+    top = BPAD - 16
+    for half in range(2):
+        cols = slice(half * BLK, half * BLK + BLK)
+        z_out[:, half * BPAD + 256 : half * BPAD + BPAD] = jnp.zeros((BPAD, 128), BF16)
+        z_out[:top, half * BPAD : half * BPAD + BLK] = z_ref[:top, cols]
+        tail[:7, half * BPAD : half * BPAD + BLK] = z_ref[top:, cols].astype(F32)
+    z_out[top:, :] = tail[...].astype(BF16)
 
 
 def pad_factors(own_ref, pair_ref, both_out, own_out):
-    both_out[...] = jnp.zeros_like(both_out)
-    both_out[0, :VIRT, :BLK] = own_ref[...]
-    both_out[1, :VIRT, :BLK] = pair_ref[...]
-    own_out[...] = jnp.zeros_like(own_out)
-    own_out[:VIRT, :BLK] = own_ref[...]
+    for out, ref in ((both_out.at[0], own_ref), (both_out.at[1], pair_ref), (own_out, own_ref)):
+        out[:, 256:] = jnp.zeros((VPAD, BPAD - 256), BF16)
+        out[VIRT - 12 :, :] = jnp.zeros((VPAD - VIRT + 12, BPAD), BF16)
+        out[:VIRT, :BLK] = ref[...]
 
 
 def scaled(block):
@@ -328,7 +330,7 @@
         pad_metric,
         shape(BPAD, TWO),
         [
-            pltpu.VMEM((BPAD, TWO), F32),
+            pltpu.VMEM((16, TWO), F32),
             pltpu.VMEM((BLK, 2 * BLK), BF16),
             pltpu.SemaphoreType.DMA,
         ],
@@ -372,7 +374,7 @@
         recv_a,
         recv_b,
         in_specs=[SMEM] + [VMEM] * 3,
-        weight=20,
+        weight=8,
     )
     z_before = move(z_here, lambda z, x, c, y: (z, x, c, y + 1))
     z_after = move(z_here, lambda z, x, c, y: (z, x, c, y - 1))
@@ -392,7 +394,6 @@
         in_specs=[SMEM] + [VMEM] * 2,
     )
     z_far = move(z_onward, lambda z, x, c, y: (z, x, c, y + 1 - 2 * c))
-    far, _ = lax.optimization_barrier((far, z_onward))
     x_parts = [x_pair, near, across(near), far, across(far)]
     dma = pltpu.SemaphoreType.DMA
     early = call(
@@ -412,6 +413,7 @@
         z_after,
         z_before,
         in_specs=[SMEM] + [VMEM] * 2 + [HBM] * 8,
+        mib=20,
     )
     left = pltpu.VMEM((8, WIN, TWO), BF16)
     half_shape = shape(TWO, TWO)

time: 123 us -> 121 us (0.984)
  waiting for transfers between devices: 40.6 us -> 45.2 us
  starting transfers between devices: 31.6 us -> 28.7 us
  Pallas kernels: 42.6 us -> 40.5 us
  local copies, waits for them, and re-layouts: 5.89 us -> 4.34 us
    ppermute x21, waiting for transfers between devices: 40.6 us -> 45.2 us  [move(): return lax.ppermute(block, BOTH, pairs)]
    ppermute x21, starting transfers between devices: 31.6 us -> 28.7 us  [move(): return lax.ppermute(block, BOTH, pairs)]
    pallas_call x16, Pallas kernels: 42.6 us -> 40.5 us  [call(): pl.pallas_call(kernel, out_shape=out_shape, in_specs=in_specs or [VMEM] *...]
    unnamed x22 -> x12, local copies, waits for them, and re-layouts: 3.87 us -> 2.33 us
  transfers between devices with their start and end apart: 21 -> 21, of which waited for: 11 -> 11; matrix products, arithmetic and copies ran while one was open for 0% -> 0% of each run, Pallas kernels for 30% -> 27%
where the time goes in v1:
time: 121 us; the launch traced here: 120 us
  waiting for transfers between devices  45.2 us (37%)
  Pallas kernels  40.5 us (33%)
  starting transfers between devices  28.7 us (24%)
  local copies, waits for them, and re-layouts  4.34 us (4%)
    ppermute x21, waiting for transfers between devices, move(): return lax.ppermute(block, BOTH, pairs)  45.2 us
    pallas_call x16, Pallas kernels, call(): pl.pallas_call(kernel, out_shape=out_shape, in_specs=in_specs or [VMEM] *...  40.5 us
    ppermute x21, starting transfers between devices, move(): return lax.ppermute(block, BOTH, pairs)  28.7 us
  transfers between devices with their start and end apart: 21, of which 11 were waited for; matrix products, arithmetic and copies ran while one was open for 0% of the time, Pallas kernels for 27%

profile of v1, /device:TPU:0, one launch (start us, length us, event | category | flops | bytes accessed | tf_op | source)
XLA Modules:
  0.0 119.6 jit_solution(15605824040207021779)
XLA Ops:
  0.0 0.0 collective-permute-start.2
  0.0 2.9 %shard_map.73.own_ref = bf16[384,768]{1,0:T(8,128)(2,1)} custom-call(bf16[375,750]{1,0:T(8,128)(2,1)} %z_hbm.1, f32[3,6]{1,0:T(4,128)} %s_ref.1), custom_call_target="tpu_custom_call" | custom-call | flops 1 | bytes 1 | tf_op jit(solution)/shard_map/pallas_call | solution.py:53
  2.9 0.1 collective-permute-done.2.pair_ref
  3.0 1.9 %shard_map.74 = (bf16[2,1536,384]{2,1,0:T(8,128)(2,1)}, bf16[1536,384]{1,0:T(8,128)(2,1)S(1)}) custom-call(bf16[1500,375]{1,0:T(8,128)(2,1)S(1)} %copy-done.1, bf16[1500,375]{1,0:T(8,128)(2,1)S(1)} %collective-permute-done.2.pair_ref), custom_call_target="tpu_custom_call" | custom-call | flops 1 | bytes 1 | tf_op jit(solution)/shard_map/pallas_call | solution.py:53
  4.9 2.0 %collective-permute-start.6 = (bf16[2,1536,384]{2,1,0:T(8,128)(2,1)}, bf16[2,1536,384]{2,1,0:T(8,128)(2,1)S(1)}, u32[]{:S(2)}, u32[]{:S(2)}) collective-permute-start(bf16[2,1536,384]{2,1,0:T(8,128)(2,1)} %get-tuple-element.53.refs_0_), channel_id=1, source_target_pairs={{0,32},{2,34},{4,36},{6,38},{8,104},{10,106},{12,108},{14,110},{1,... | collective-permute-start | bytes 7077896 | tf_op jit(solution)/shard_map/ppermute | solution.py:33
  6.9 1.5 %collective-permute-start = (bf16[384,768]{1,0:T(8,128)(2,1)}, bf16[384,768]{1,0:T(8,128)(2,1)}, u32[]{:S(2)}, u32[]{:S(2)}) collective-permute-start(bf16[384,768]{1,0:T(8,128)(2,1)} %shard_map.73.own_ref), channel_id=1, source_target_pairs={{0,1},{2,3},{4,5},{6,7},{8,9},{10,11},{12,13},{14,15},{1,17},{3,19... | collective-permute-start | bytes 1769480 | tf_op jit(solution)/shard_map/ppermute | solution.py:33
  8.4 1.5 %collective-permute-start.1 = (bf16[384,768]{1,0:T(8,128)(2,1)}, bf16[384,768]{1,0:T(8,128)(2,1)}, u32[]{:S(2)}, u32[]{:S(2)}) collective-permute-start(bf16[384,768]{1,0:T(8,128)(2,1)} %shard_map.73.own_ref), channel_id=1, source_target_pairs={{1,16},{3,18},{5,20},{7,22},{9,24},{11,26},{13,28},{15,30},{16,1},... | collective-permute-start | bytes 1769480 | tf_op jit(solution)/shard_map/ppermute | solution.py:33
  9.9 0.1 stack.80.info
  10.0 0.0 copy-start
  10.0 2.3 %copy-done = bf16[1,1500,1500]{2,1,0:T(8,128)(2,1)S(1)} copy-done((bf16[1,1500,1500]{2,1,0:T(8,128)(2,1)S(1)}, bf16[1,1500,1500]{2,1,0:T(8,128)(2,1)}, u32[]{:S(2)}) %copy-start) | copy-done | bytes 4500024
  12.3 2.9 %shard_map.75 = (bf16[384,1536]{1,0:T(8,128)(2,1)S(1)}, bf16[2,8,96,384]{3,2,1,0:T(8,128)(2,1)S(1)}) custom-call(s32[16]{0:T(128)S(1)} %stack.80.info, bf16[1536,384]{1,0:T(8,128)(2,1)S(1)} %get-tuple-element.52.x_ref, bf16[1,1500,1500]{2,1,0:T(8,128)(2,1)S(1)} %copy-done), custom_call_target="tpu_custom_call" | custom-call | flops 1 | bytes 1 | tf_op jit(solution)/shard_map/pallas_call | solution.py:53
  15.1 8.6 %collective-permute-done.a_ref = bf16[384,768]{1,0:T(8,128)(2,1)} collective-permute-done((bf16[384,768]{1,0:T(8,128)(2,1)}, bf16[384,768]{1,0:T(8,128)(2,1)}, u32[]{:S(2)}, u32[]{:S(2)}) %collective-permute-start) | collective-permute-done | bytes 589856 | tf_op jit(solution)/shard_map/ppermute | solution.py:33
  23.8 0.0 collective-permute-done.1.b_ref
  23.8 2.8 %collective-permute-start.5 = (bf16[1536,384]{1,0:T(8,128)(2,1)S(1)}, bf16[1536,384]{1,0:T(8,128)(2,1)S(1)}, u32[]{:S(2)}, u32[]{:S(2)}) collective-permute-start(bf16[1536,384]{1,0:T(8,128)(2,1)S(1)} %get-tuple-element.52.x_ref), channel_id=1, source_target_pairs={{0,17},{2,19},{4,21},{6,23},{8,25},{10,27},{12,29},{14,31},{1,16},... | collective-permute-start | bytes 3538952 | tf_op jit(solution)/shard_map/ppermute | solution.py:33
  26.6 1.5 %shard_map.76.refs_5_ = bf16[2,384,768]{2,1,0:T(8,128)(2,1)S(1)} custom-call(s32[16]{0:T(128)S(1)} %stack.80.info, bf16[384,768]{1,0:T(8,128)(2,1)} %shard_map.73.own_ref, bf16[384,768]{1,0:T(8,128)(2,1)} %collective-permute-done.a_ref, bf16[384,768]{1,0:T(8,128)(2,1)} %collective-permute-done.1.b_ref), custom_call_target="tpu_custom_call" | custom-call | flops 8000000000 | bytes 8000001 | tf_op jit(solution)/shard_map/pallas_call | solution.py:53
  28.1 1.6 %collective-permute-start.3 = (bf16[2,384,768]{2,1,0:T(8,128)(2,1)S(1)}, bf16[2,384,768]{2,1,0:T(8,128)(2,1)S(1)}, u32[]{:S(2)}, u32[]{:S(2)}) collective-permute-start(bf16[2,384,768]{2,1,0:T(8,128)(2,1)S(1)} %shard_map.76.refs_5_), channel_id=1, source_target_pairs={{0,2},{2,4},{4,6},{6,0},{8,10},{10,12},{12,14},{14,8},{1,3},{3,5},... | collective-permute-start | bytes 3538952 | tf_op jit(solution)/shard_map/ppermute | solution.py:33
  29.8 1.7 %collective-permute-start.4 = (bf16[2,384,768]{2,1,0:T(8,128)(2,1)S(1)}, bf16[2,384,768]{2,1,0:T(8,128)(2,1)S(1)}, u32[]{:S(2)}, u32[]{:S(2)}) collective-permute-start(bf16[2,384,768]{2,1,0:T(8,128)(2,1)S(1)} %shard_map.76.refs_5_), channel_id=1, source_target_pairs={{0,6},{2,0},{4,2},{6,4},{8,14},{10,8},{12,10},{14,12},{1,7},{3,1},... | collective-permute-start | bytes 3538952 | tf_op jit(solution)/shard_map/ppermute | solution.py:33
  31.4 4.6 %collective-permute-done.6.refs_1_ = bf16[2,1536,384]{2,1,0:T(8,128)(2,1)S(1)} collective-permute-done((bf16[2,1536,384]{2,1,0:T(8,128)(2,1)}, bf16[2,1536,384]{2,1,0:T(8,128)(2,1)S(1)}, u32[]{:S(2)}, u32[]{:S(2)}) %collective-permute-start.6) | collective-permute-done | bytes 2359328 | tf_op jit(solution)/shard_map/ppermute | solution.py:33
  36.0 0.1 slice_bitcast_fusion
  36.2 0.1 collective-permute-start.8
  36.3 2.3 %collective-permute-start.7 = (bf16[2,1536,384]{2,1,0:T(8,128)(2,1)S(1)}, bf16[2,1536,384]{2,1,0:T(8,128)(2,1)S(1)}, u32[]{:S(2)}, u32[]{:S(2)}) collective-permute-start(bf16[2,1536,384]{2,1,0:T(8,128)(2,1)S(1)} %collective-permute-done.6.refs_1_), channel_id=1, source_target_pairs={{0,8},{2,10},{4,12},{6,14},{8,0},{10,2},{12,4},{14,6},{1,9},{3,11}... | collective-permute-start | bytes 7077896 | tf_op jit(solution)/shard_map/ppermute | solution.py:33
  38.6 0.3 shard_map.77.amp_ref
  38.9 15.0 %collective-permute-done.5.x_ref = bf16[1536,384]{1,0:T(8,128)(2,1)S(1)} collective-permute-done((bf16[1536,384]{1,0:T(8,128)(2,1)S(1)}, bf16[1536,384]{1,0:T(8,128)(2,1)S(1)}, u32[]{:S(2)}, u32[]{:S(2)}) %collective-permute-start.5) | collective-permute-done | bytes 1179680 | tf_op jit(solution)/shard_map/ppermute | solution.py:33
  53.9 2.9 %shard_map.78 = (bf16[384,1536]{1,0:T(8,128)(2,1)S(1)}, bf16[2,8,96,384]{3,2,1,0:T(8,128)(2,1)S(1)}) custom-call(s32[16]{0:T(128)S(1)} %stack.80.info, bf16[1536,384]{1,0:T(8,128)(2,1)S(1)} %collective-permute-done.5.x_ref, bf16[1,1500,1500]{2,1,0:T(8,128)(2,1)S(1)} %shard_map.77.amp_ref), custom_call_target="tpu_custom_call" | custom-call | flops 10000000000 | bytes 10000001 | tf_op jit(solution)/shard_map/pallas_call | solution.py:53
  56.8 1.3 %collective-permute-done.3.first_ref.refs_7_ = bf16[2,384,768]{2,1,0:T(8,128)(2,1)S(1)} collective-permute-done((bf16[2,384,768]{2,1,0:T(8,128)(2,1)S(1)}, bf16[2,384,768]{2,1,0:T(8,128)(2,1)S(1)}, u32[]{:S(2)}, u32[]{:S(2)}) %collective-permute-start.3) | collective-permute-done | bytes 1179680 | tf_op jit(solution)/shard_map/ppermute | solution.py:33
  58.0 0.0 collective-permute-done.4.second_ref.refs_6_
  58.1 0.0 collective-permute-done.8.refs_3_
  58.1 0.0 collective-permute-start.9
  58.1 0.6 shard_map.79
  58.7 1.6 %collective-permute-start.10 = (bf16[2,384,768]{2,1,0:T(8,128)(2,1)S(1)}, bf16[2,384,768]{2,1,0:T(8,128)(2,1)S(1)}, u32[]{:S(2)}, u32[]{:S(2)}) collective-permute-start(bf16[2,384,768]{2,1,0:T(8,128)(2,1)S(1)} %shard_map.79), channel_id=1, source_target_pairs={{0,2},{2,4},{4,6},{6,0},{8,14},{10,8},{12,10},{14,12},{1,3},{3,5},... | collective-permute-start | bytes 3538952 | tf_op jit(solution)/shard_map/ppermute | solution.py:33
  60.4 0.6 collective-permute-done.9.refs_4_
  60.9 0.0 collective-permute-done.7.refs_2_
  60.9 15.4 %shard_map.80.refs_6_.early_ref = f32[768,1536]{1,0:T(8,128)S(1)} custom-call(s32[16]{0:T(128)S(1)} %stack.80.info, bf16[384,1536]{1,0:T(8,128)(2,1)S(1)} %get-tuple-element.48.h0_ref, bf16[384,1536]{1,0:T(8,128)(2,1)S(1)} %get-tuple-element.58.h1_ref, bf16[2,1536,384]{2,1,0:T(8,128)(2,1)} %get-tuple-element.53.refs_0_, ...), custom_call_target="tpu_custom_call" | custom-call | flops 1 | bytes 1 | tf_op jit(solution)/shard_map/pallas_call | solution.py:53
  76.4 0.0 collective-permute-done.10.refs_5_
  76.4 5.6 %shard_map.81 = (bf16[768,768]{1,0:T(8,128)(2,1)S(1)}, bf16[1536,768]{1,0:T(8,128)(2,1)S(1)}, bf16[768,768]{1,0:T(8,128)(2,1)S(1)}, bf16[768,768]{1,0:T(8,128)(2,1)S(1)}) custom-call(s32[16]{0:T(128)S(1)} %stack.80.info, bf16[384,1536]{1,0:T(8,128)(2,1)S(1)} %get-tuple-element.48.h0_ref, bf16[384,1536]{1,0:T(8,128)(2,1)S(1)} %get-tuple-element.58.h1_ref, ...), custom_call_target="tpu_custom_call" | custom-call | flops 1 | bytes 1 | tf_op jit(solution)/shard_map/pallas_call | solution.py:53
  82.0 1.2 collective-permute-start.11
  83.1 2.9 %shard_map.84 = (bf16[768,768]{1,0:T(8,128)(2,1)S(1)}, bf16[768,768]{1,0:T(8,128)(2,1)S(1)}) custom-call(f32[768,1536]{1,0:T(8,128)S(1)} %shard_map.80.refs_6_.early_ref, bf16[768,768]{1,0:T(8,128)(2,1)S(1)} %get-tuple-element.68.newest_ref, bf16[1536,768]{1,0:T(8,128)(2,1)S(1)} %get-tuple-element.69.xn_ref, ...), custom_call_target="tpu_custom_call" | custom-call | flops 1 | bytes 1 | tf_op jit(solution)/shard_map/pallas_call | solution.py:53
  86.1 0.3 collective-permute-start.13
  86.4 1.2 %shard_map.82 = (f32[384,768]{1,0:T(8,128)S(1)}, bf16[384,768]{1,0:T(8,128)(2,1)S(1)}) custom-call(bf16[768,768]{1,0:T(8,128)(2,1)S(1)} %get-tuple-element.63.back_ref, bf16[2,8,96,384]{3,2,1,0:T(8,128)(2,1)S(1)} %get-tuple-element.61.refs_7_.w0_ref, bf16[2,8,96,384]{3,2,1,0:T(8,128)(2,1)S(1)} %get-tuple-element.62.refs_8_.w1_ref, ...), custom_call_target="tpu_custom_call" | custom-call | flops 1 | bytes 1 | tf_op jit(solution)/shard_map/pallas_call | solution.py:53
  87.6 3.5 %collective-permute-start.12 = (bf16[384,768]{1,0:T(8,128)(2,1)S(1)}, bf16[384,768]{1,0:T(8,128)(2,1)S(1)}, u32[]{:S(2)}, u32[]{:S(2)}) collective-permute-start(bf16[384,768]{1,0:T(8,128)(2,1)S(1)} %get-tuple-element.66), channel_id=1, source_target_pairs={{0,16},{2,18},{4,20},{6,22},{8,24},{10,26},{12,28},{14,30},{1,17},... | collective-permute-start | bytes 1769480 | tf_op jit(solution)/shard_map/ppermute | solution.py:33
  91.1 0.0 collective-permute-done.13.got_ref
  91.2 1.2 %shard_map.85 = (f32[2,96,768]{2,1,0:T(8,128)S(1)}, bf16[2,96,768]{2,1,0:T(8,128)(2,1)S(1)}, bf16[2,96,768]{2,1,0:T(8,128)(2,1)S(1)}, bf16[2,96,768]{2,1,0:T(8,128)(2,1)S(1)}) custom-call(bf16[768,768]{1,0:T(8,128)(2,1)S(1)} %get-tuple-element.70.back_ref, bf16[2,8,96,384]{3,2,1,0:T(8,128)(2,1)S(1)} %get-tuple-element.61.refs_7_.w0_ref, ...), custom_call_target="tpu_custom_call" | custom-call | flops 1 | bytes 1 | tf_op jit(solution)/shard_map/pallas_call | solution.py:53
  92.4 0.0 copy-start.3
  92.4 0.1 collective-permute-start.14
  92.5 2.2 %collective-permute-start.15 = (bf16[2,96,768]{2,1,0:T(8,128)(2,1)S(1)}, bf16[2,96,768]{2,1,0:T(8,128)(2,1)S(1)}, u32[]{:S(2)}, u32[]{:S(2)}) collective-permute-start(bf16[2,96,768]{2,1,0:T(8,128)(2,1)S(1)} %get-tuple-element.73), channel_id=1, source_target_pairs={{0,64},{2,66},{4,68},{6,70},{8,72},{10,74},{12,76},{14,78},{1,65},... | collective-permute-start | bytes 884744 | tf_op jit(solution)/shard_map/ppermute | solution.py:33
  94.6 1.1 collective-permute-start.16
  95.7 9.4 %collective-permute-done.12.got_ref = bf16[384,768]{1,0:T(8,128)(2,1)S(1)} collective-permute-done((bf16[384,768]{1,0:T(8,128)(2,1)S(1)}, bf16[384,768]{1,0:T(8,128)(2,1)S(1)}, u32[]{:S(2)}, u32[]{:S(2)}) %collective-permute-start.12) | collective-permute-done | bytes 589856 | tf_op jit(solution)/shard_map/ppermute | solution.py:33
  105.1 0.1 shard_map.83
  105.2 0.1 collective-permute-start.17
  105.3 2.5 %collective-permute-start.18 = (bf16[96,768]{1,0:T(8,128)(2,1)S(1)}, bf16[96,768]{1,0:T(8,128)(2,1)S(1)}, u32[]{:S(2)}, u32[]{:S(2)}) collective-permute-start(bf16[96,768]{1,0:T(8,128)(2,1)S(1)} %get-tuple-element.77), channel_id=1, source_target_pairs={{0,64},{2,66},{4,68},{6,70},{8,72},{10,74},{12,76},{14,78},{1,65},... | collective-permute-start | bytes 442376 | tf_op jit(solution)/shard_map/ppermute | solution.py:33
  107.8 1.4 %collective-permute-done.14.got_1 = bf16[2,96,768]{2,1,0:T(8,128)(2,1)S(1)} collective-permute-done((bf16[2,96,768]{2,1,0:T(8,128)(2,1)S(1)}, bf16[2,96,768]{2,1,0:T(8,128)(2,1)S(1)}, u32[]{:S(2)}, u32[]{:S(2)}) %collective-permute-start.14) | collective-permute-done | bytes 294944 | tf_op jit(solution)/shard_map/ppermute | solution.py:33
  109.3 0.0 collective-permute-start.19
  109.9 0.1 pad_add_fusion.numbers
  110.0 0.1 shard_map.87
  110.2 0.0 copy-start.2
  110.2 2.6 %collective-permute-start.20 = (bf16[96,768]{1,0:T(8,128)(2,1)S(1)}, bf16[96,768]{1,0:T(8,128)(2,1)S(1)}, u32[]{:S(2)}, u32[]{:S(2)}) collective-permute-start(bf16[96,768]{1,0:T(8,128)(2,1)S(1)} %get-tuple-element.84), channel_id=1, source_target_pairs={{0,16},{2,18},{4,20},{6,22},{8,24},{10,26},{12,28},{14,30},{1,17},... | collective-permute-start | bytes 442376 | tf_op jit(solution)/shard_map/ppermute | solution.py:33
  112.8 2.7 %collective-permute-done.17.refs_0_ = bf16[96,768]{1,0:T(8,128)(2,1)S(1)} collective-permute-done((bf16[96,768]{1,0:T(8,128)(2,1)S(1)}, bf16[96,768]{1,0:T(8,128)(2,1)S(1)}, u32[]{:S(2)}, u32[]{:S(2)}) %collective-permute-start.17) | collective-permute-done | bytes 147488 | tf_op jit(solution)/shard_map/ppermute | solution.py:33
  115.4 0.0 collective-permute-done.18.refs_1_
  115.4 0.7 collective-permute-done.19.refs_2_
  116.1 0.1 shard_map.86.a_ref
  116.2 0.7 collective-permute-done.20.b1_ref
  116.9 0.9 shard_map.88
  117.8 0.9 reshape.11
  118.8 0.8 slice.9
  (13 shorter events, 0.0 us)
Async XLA Ops:
  0.0 3.0 %copy-start.1 = (bf16[1500,375]{1,0:T(8,128)(2,1)S(1)}, bf16[1500,375]{1,0:T(8,128)(2,1)}, u32[]{:S(2)}) copy-start(bf16[1500,375]{1,0:T(8,128)(2,1)} %own_ref.1) | copy-start | bytes 3375004
  0.0 3.0 %collective-permute-start.2 = (bf16[1500,375]{1,0:T(8,128)(2,1)}, bf16[1500,375]{1,0:T(8,128)(2,1)S(1)}, u32[]{:S(2)}, u32[]{:S(2)}) collective-permute-start(bf16[1500,375]{1,0:T(8,128)(2,1)} %own_ref.1), channel_id=1, source_target_pairs={{0,8},{2,10},{4,12},{6,14},{8,0},{10,2},{12,4},{14,6},{1,9},{3,11}... | collective-permute-start | bytes 3375008 | tf_op jit(solution)/shard_map/ppermute | solution.py:33
  4.9 31.2 %collective-permute-start.6 = (bf16[2,1536,384]{2,1,0:T(8,128)(2,1)}, bf16[2,1536,384]{2,1,0:T(8,128)(2,1)S(1)}, u32[]{:S(2)}, u32[]{:S(2)}) collective-permute-start(bf16[2,1536,384]{2,1,0:T(8,128)(2,1)} %get-tuple-element.53.refs_0_), channel_id=1, source_target_pairs={{0,32},{2,34},{4,36},{6,38},{8,104},{10,106},{12,108},{14,110},{1,... | collective-permute-start | bytes 7077896 | tf_op jit(solution)/shard_map/ppermute | solution.py:33
  6.9 16.9 %collective-permute-start = (bf16[384,768]{1,0:T(8,128)(2,1)}, bf16[384,768]{1,0:T(8,128)(2,1)}, u32[]{:S(2)}, u32[]{:S(2)}) collective-permute-start(bf16[384,768]{1,0:T(8,128)(2,1)} %shard_map.73.own_ref), channel_id=1, source_target_pairs={{0,1},{2,3},{4,5},{6,7},{8,9},{10,11},{12,13},{14,15},{1,17},{3,19... | collective-permute-start | bytes 1769480 | tf_op jit(solution)/shard_map/ppermute | solution.py:33
  8.4 15.4 %collective-permute-start.1 = (bf16[384,768]{1,0:T(8,128)(2,1)}, bf16[384,768]{1,0:T(8,128)(2,1)}, u32[]{:S(2)}, u32[]{:S(2)}) collective-permute-start(bf16[384,768]{1,0:T(8,128)(2,1)} %shard_map.73.own_ref), channel_id=1, source_target_pairs={{1,16},{3,18},{5,20},{7,22},{9,24},{11,26},{13,28},{15,30},{16,1},... | collective-permute-start | bytes 1769480 | tf_op jit(solution)/shard_map/ppermute | solution.py:33
  10.0 2.3 %copy-start = (bf16[1,1500,1500]{2,1,0:T(8,128)(2,1)S(1)}, bf16[1,1500,1500]{2,1,0:T(8,128)(2,1)}, u32[]{:S(2)}) copy-start(bf16[1,1500,1500]{2,1,0:T(8,128)(2,1)} %in_ref) | copy-start | bytes 13500004
  23.8 14.8 %slice-start = ((s8[4620288]{0:T(1024)(128)(4,1)}), s8[4194304]{0:T(1024)(128)(4,1)S(1)}, s32[]{:S(2)}) async-start(s8[4620288]{0:T(1024)(128)(4,1)} %bitcast.20), calls=%async_computation | async-start | bytes 8388608
  23.8 14.8 %slice-start.1 = ((s8[4620288]{0:T(1024)(128)(4,1)}), s8[425984]{0:T(1024)(128)(4,1)S(1)}, s32[]{:S(2)}) async-start(s8[4620288]{0:T(1024)(128)(4,1)} %bitcast.20), calls=%async_computation.1 | async-start | bytes 851968
  23.8 30.1 %collective-permute-start.5 = (bf16[1536,384]{1,0:T(8,128)(2,1)S(1)}, bf16[1536,384]{1,0:T(8,128)(2,1)S(1)}, u32[]{:S(2)}, u32[]{:S(2)}) collective-permute-start(bf16[1536,384]{1,0:T(8,128)(2,1)S(1)} %get-tuple-element.52.x_ref), channel_id=1, source_target_pairs={{0,17},{2,19},{4,21},{6,23},{8,25},{10,27},{12,29},{14,31},{1,16},... | collective-permute-start | bytes 3538952 | tf_op jit(solution)/shard_map/ppermute | solution.py:33
  28.1 29.9 %collective-permute-start.3 = (bf16[2,384,768]{2,1,0:T(8,128)(2,1)S(1)}, bf16[2,384,768]{2,1,0:T(8,128)(2,1)S(1)}, u32[]{:S(2)}, u32[]{:S(2)}) collective-permute-start(bf16[2,384,768]{2,1,0:T(8,128)(2,1)S(1)} %shard_map.76.refs_5_), channel_id=1, source_target_pairs={{0,2},{2,4},{4,6},{6,0},{8,10},{10,12},{12,14},{14,8},{1,3},{3,5},... | collective-permute-start | bytes 3538952 | tf_op jit(solution)/shard_map/ppermute | solution.py:33
  29.8 28.3 %collective-permute-start.4 = (bf16[2,384,768]{2,1,0:T(8,128)(2,1)S(1)}, bf16[2,384,768]{2,1,0:T(8,128)(2,1)S(1)}, u32[]{:S(2)}, u32[]{:S(2)}) collective-permute-start(bf16[2,384,768]{2,1,0:T(8,128)(2,1)S(1)} %shard_map.76.refs_5_), channel_id=1, source_target_pairs={{0,6},{2,0},{4,2},{6,4},{8,14},{10,8},{12,10},{14,12},{1,7},{3,1},... | collective-permute-start | bytes 3538952 | tf_op jit(solution)/shard_map/ppermute | solution.py:33
  36.2 21.9 %collective-permute-start.8 = (bf16[1536,384]{1,0:T(8,128)(2,1)S(1)}, bf16[1536,384]{1,0:T(8,128)(2,1)S(1)}, u32[]{:S(2)}, u32[]{:S(2)}) collective-permute-start(bf16[1536,384]{1,0:T(8,128)(2,1)S(1)} %slice_bitcast_fusion), channel_id=1, source_target_pairs={{0,32},{2,34},{4,36},{6,38},{8,104},{10,106},{12,108},{14,110},{1,... | collective-permute-start | bytes 3538952 | tf_op jit(solution)/shard_map/ppermute | solution.py:33
  36.3 24.7 %collective-permute-start.7 = (bf16[2,1536,384]{2,1,0:T(8,128)(2,1)S(1)}, bf16[2,1536,384]{2,1,0:T(8,128)(2,1)S(1)}, u32[]{:S(2)}, u32[]{:S(2)}) collective-permute-start(bf16[2,1536,384]{2,1,0:T(8,128)(2,1)S(1)} %collective-permute-done.6.refs_1_), channel_id=1, source_target_pairs={{0,8},{2,10},{4,12},{6,14},{8,0},{10,2},{12,4},{14,6},{1,9},{3,11}... | collective-permute-start | bytes 7077896 | tf_op jit(solution)/shard_map/ppermute | solution.py:33
  58.1 2.8 %collective-permute-start.9 = (bf16[1536,384]{1,0:T(8,128)(2,1)S(1)}, bf16[1536,384]{1,0:T(8,128)(2,1)S(1)}, u32[]{:S(2)}, u32[]{:S(2)}) collective-permute-start(bf16[1536,384]{1,0:T(8,128)(2,1)S(1)} %collective-permute-done.8.refs_3_), channel_id=1, source_target_pairs={{0,8},{2,10},{4,12},{6,14},{8,0},{10,2},{12,4},{14,6},{1,9},{3,11}... | collective-permute-start | bytes 3538952 | tf_op jit(solution)/shard_map/ppermute | solution.py:33
  58.7 17.6 %collective-permute-start.10 = (bf16[2,384,768]{2,1,0:T(8,128)(2,1)S(1)}, bf16[2,384,768]{2,1,0:T(8,128)(2,1)S(1)}, u32[]{:S(2)}, u32[]{:S(2)}) collective-permute-start(bf16[2,384,768]{2,1,0:T(8,128)(2,1)S(1)} %shard_map.79), channel_id=1, source_target_pairs={{0,2},{2,4},{4,6},{6,0},{8,14},{10,8},{12,10},{14,12},{1,3},{3,5},... | collective-permute-start | bytes 3538952 | tf_op jit(solution)/shard_map/ppermute | solution.py:33
  82.0 4.4 %collective-permute-start.11 = (bf16[768,768]{1,0:T(8,128)(2,1)S(1)}, bf16[768,768]{1,0:T(8,128)(2,1)S(1)}, u32[]{:S(2)}, u32[]{:S(2)}) collective-permute-start(bf16[768,768]{1,0:T(8,128)(2,1)S(1)} %get-tuple-element.64), channel_id=1, source_target_pairs={{0,8},{2,10},{4,12},{6,14},{8,0},{10,2},{12,4},{14,6},{1,9},{3,11}... | collective-permute-start | bytes 3538952 | tf_op jit(solution)/shard_map/ppermute | solution.py:33
  86.1 5.1 %collective-permute-start.13 = (bf16[768,768]{1,0:T(8,128)(2,1)S(1)}, bf16[768,768]{1,0:T(8,128)(2,1)S(1)}, u32[]{:S(2)}, u32[]{:S(2)}) collective-permute-start(bf16[768,768]{1,0:T(8,128)(2,1)S(1)} %get-tuple-element.71), channel_id=1, source_target_pairs={{0,8},{2,10},{4,12},{6,14},{8,0},{10,2},{12,4},{14,6},{1,9},{3,11}... | collective-permute-start | bytes 3538952 | tf_op jit(solution)/shard_map/ppermute | solution.py:33
  87.6 17.5 %collective-permute-start.12 = (bf16[384,768]{1,0:T(8,128)(2,1)S(1)}, bf16[384,768]{1,0:T(8,128)(2,1)S(1)}, u32[]{:S(2)}, u32[]{:S(2)}) collective-permute-start(bf16[384,768]{1,0:T(8,128)(2,1)S(1)} %get-tuple-element.66), channel_id=1, source_target_pairs={{0,16},{2,18},{4,20},{6,22},{8,24},{10,26},{12,28},{14,30},{1,17},... | collective-permute-start | bytes 1769480 | tf_op jit(solution)/shard_map/ppermute | solution.py:33
  92.4 17.5 %copy-start.3 = (f32[1500]{0:T(1024)S(1)}, f32[1500]{0:T(1024)}, u32[]{:S(2)}) copy-start(f32[1500]{0:T(1024)} %param.12) | copy-start | bytes 18004
  92.4 16.9 %collective-permute-start.14 = (bf16[2,96,768]{2,1,0:T(8,128)(2,1)S(1)}, bf16[2,96,768]{2,1,0:T(8,128)(2,1)S(1)}, u32[]{:S(2)}, u32[]{:S(2)}) collective-permute-start(bf16[2,96,768]{2,1,0:T(8,128)(2,1)S(1)} %get-tuple-element.72), channel_id=1, source_target_pairs={{0,32},{2,34},{4,36},{6,38},{8,40},{10,42},{12,44},{14,46},{1,33},... | collective-permute-start | bytes 884744 | tf_op jit(solution)/shard_map/ppermute | solution.py:33
  92.5 17.5 %collective-permute-start.15 = (bf16[2,96,768]{2,1,0:T(8,128)(2,1)S(1)}, bf16[2,96,768]{2,1,0:T(8,128)(2,1)S(1)}, u32[]{:S(2)}, u32[]{:S(2)}) collective-permute-start(bf16[2,96,768]{2,1,0:T(8,128)(2,1)S(1)} %get-tuple-element.73), channel_id=1, source_target_pairs={{0,64},{2,66},{4,68},{6,70},{8,72},{10,74},{12,76},{14,78},{1,65},... | collective-permute-start | bytes 884744 | tf_op jit(solution)/shard_map/ppermute | solution.py:33
  94.6 15.4 %collective-permute-start.16 = (bf16[2,96,768]{2,1,0:T(8,128)(2,1)S(1)}, bf16[2,96,768]{2,1,0:T(8,128)(2,1)S(1)}, u32[]{:S(2)}, u32[]{:S(2)}) collective-permute-start(bf16[2,96,768]{2,1,0:T(8,128)(2,1)S(1)} %get-tuple-element.74), channel_id=1, source_target_pairs={{0,96},{2,98},{4,100},{6,102},{8,104},{10,106},{12,108},{14,110},{... | collective-permute-start | bytes 884744 | tf_op jit(solution)/shard_map/ppermute | solution.py:33
  105.2 10.2 %collective-permute-start.17 = (bf16[96,768]{1,0:T(8,128)(2,1)S(1)}, bf16[96,768]{1,0:T(8,128)(2,1)S(1)}, u32[]{:S(2)}, u32[]{:S(2)}) collective-permute-start(bf16[96,768]{1,0:T(8,128)(2,1)S(1)} %get-tuple-element.76), channel_id=1, source_target_pairs={{0,32},{2,34},{4,36},{6,38},{8,40},{10,42},{12,44},{14,46},{1,33},... | collective-permute-start | bytes 442376 | tf_op jit(solution)/shard_map/ppermute | solution.py:33
  105.3 10.1 %collective-permute-start.18 = (bf16[96,768]{1,0:T(8,128)(2,1)S(1)}, bf16[96,768]{1,0:T(8,128)(2,1)S(1)}, u32[]{:S(2)}, u32[]{:S(2)}) collective-permute-start(bf16[96,768]{1,0:T(8,128)(2,1)S(1)} %get-tuple-element.77), channel_id=1, source_target_pairs={{0,64},{2,66},{4,68},{6,70},{8,72},{10,74},{12,76},{14,78},{1,65},... | collective-permute-start | bytes 442376 | tf_op jit(solution)/shard_map/ppermute | solution.py:33
  109.3 6.9 %collective-permute-start.19 = (bf16[96,768]{1,0:T(8,128)(2,1)S(1)}, bf16[96,768]{1,0:T(8,128)(2,1)S(1)}, u32[]{:S(2)}, u32[]{:S(2)}) collective-permute-start(bf16[96,768]{1,0:T(8,128)(2,1)S(1)} %get-tuple-element.78), channel_id=1, source_target_pairs={{0,96},{2,98},{4,100},{6,102},{8,104},{10,106},{12,108},{14,110},{... | collective-permute-start | bytes 442376 | tf_op jit(solution)/shard_map/ppermute | solution.py:33
  110.2 6.7 %copy-start.2 = (f32[150]{0:T(256)S(1)}, f32[150]{0:T(256)}, u32[]{:S(2)}) copy-start(f32[150]{0:T(256)} %param.13) | copy-start | bytes 1804
  110.2 6.7 %collective-permute-start.20 = (bf16[96,768]{1,0:T(8,128)(2,1)S(1)}, bf16[96,768]{1,0:T(8,128)(2,1)S(1)}, u32[]{:S(2)}, u32[]{:S(2)}) collective-permute-start(bf16[96,768]{1,0:T(8,128)(2,1)S(1)} %get-tuple-element.84), channel_id=1, source_target_pairs={{0,16},{2,18},{4,20},{6,22},{8,24},{10,26},{12,28},{14,30},{1,17},... | collective-permute-start | bytes 442376 | tf_op jit(solution)/shard_map/ppermute | solution.py:33

commit v2 on v1

--- a/solution.py
+++ b/solution.py
@@ -468,11 +468,11 @@
         got_b,
         in_specs=[VMEM, HBM, HBM, VMEM],
     )
-    from_z = [move(send, to_z[dz]) for dz, send in enumerate(sends_b, start=1)]
+    from_z = [move(sends_b[dz - 1], to_z[dz]) for dz in (2, 1, 3)]
     total_a, *sends_a = call(
         then_z, tuple([shape(WIN, TWO, dtype=F32)] + [shape(WIN, TWO)] * 3), [], own_a, from_x
     )
-    last_z = [move(send, to_z[dz]) for dz, send in enumerate(sends_a, start=1)]
+    last_z = [move(sends_a[dz - 1], to_z[dz]) for dz in (2, 1, 3)]
     total_a, from_z = lax.optimization_barrier((total_a, from_z))
     total_b, send_b = call(
         then_x, (shape(WIN, TWO, dtype=F32), shape(WIN, TWO)), [], own_b, *from_z

time: 121 us -> 120 us (level)
  waiting for transfers between devices: 45.2 us -> 43.3 us
  starting transfers between devices: 28.7 us -> 30.3 us
    ppermute x21, waiting for transfers between devices: 45.2 us -> 43.3 us  [move(): return lax.ppermute(block, BOTH, pairs)]
    ppermute x21, starting transfers between devices: 28.7 us -> 30.3 us  [move(): return lax.ppermute(block, BOTH, pairs)]
  transfers between devices with their start and end apart: 21 -> 21, of which waited for: 11 -> 10; matrix products, arithmetic and copies ran while one was open for 0% -> 0% of each run, Pallas kernels for 27% -> 27%
where the time goes in v2:
time: 120 us; the launch traced here: 119 us
  waiting for transfers between devices  43.3 us (36%)
  Pallas kernels  40.5 us (34%)
  starting transfers between devices  30.3 us (25%)
  local copies, waits for them, and re-layouts  4.34 us (4%)
    ppermute x21, waiting for transfers between devices, move(): return lax.ppermute(block, BOTH, pairs)  43.3 us
    pallas_call x16, Pallas kernels, call(): pl.pallas_call(kernel, out_shape=out_shape, in_specs=in_specs or [VMEM] *...  40.5 us
    ppermute x21, starting transfers between devices, move(): return lax.ppermute(block, BOTH, pairs)  30.3 us
  transfers between devices with their start and end apart: 21, of which 10 were waited for; matrix products, arithmetic and copies ran while one was open for 0% of the time, Pallas kernels for 27%

profile of v2, /device:TPU:0, one launch (start us, length us, event | category | flops | bytes accessed | tf_op | source)
XLA Modules:
  0.0 119.3 jit_solution(16103041788348055695)
XLA Ops:
  0.0 0.0 collective-permute-start.2
  0.0 2.9 %shard_map.73.own_ref = bf16[384,768]{1,0:T(8,128)(2,1)} custom-call(bf16[375,750]{1,0:T(8,128)(2,1)} %z_hbm.1, f32[3,6]{1,0:T(4,128)} %s_ref.1), custom_call_target="tpu_custom_call" | custom-call | flops 1 | bytes 1 | tf_op jit(solution)/shard_map/pallas_call | solution.py:53
  2.9 0.1 collective-permute-done.2.pair_ref
  3.0 1.9 %shard_map.74 = (bf16[2,1536,384]{2,1,0:T(8,128)(2,1)}, bf16[1536,384]{1,0:T(8,128)(2,1)S(1)}) custom-call(bf16[1500,375]{1,0:T(8,128)(2,1)S(1)} %copy-done.1, bf16[1500,375]{1,0:T(8,128)(2,1)S(1)} %collective-permute-done.2.pair_ref), custom_call_target="tpu_custom_call" | custom-call | flops 1 | bytes 1 | tf_op jit(solution)/shard_map/pallas_call | solution.py:53
  4.9 2.0 %collective-permute-start.6 = (bf16[2,1536,384]{2,1,0:T(8,128)(2,1)}, bf16[2,1536,384]{2,1,0:T(8,128)(2,1)S(1)}, u32[]{:S(2)}, u32[]{:S(2)}) collective-permute-start(bf16[2,1536,384]{2,1,0:T(8,128)(2,1)} %get-tuple-element.53.refs_0_), channel_id=1, source_target_pairs={{0,32},{2,34},{4,36},{6,38},{8,104},{10,106},{12,108},{14,110},{1,... | collective-permute-start | bytes 7077896 | tf_op jit(solution)/shard_map/ppermute | solution.py:33
  6.9 1.5 %collective-permute-start = (bf16[384,768]{1,0:T(8,128)(2,1)}, bf16[384,768]{1,0:T(8,128)(2,1)}, u32[]{:S(2)}, u32[]{:S(2)}) collective-permute-start(bf16[384,768]{1,0:T(8,128)(2,1)} %shard_map.73.own_ref), channel_id=1, source_target_pairs={{0,1},{2,3},{4,5},{6,7},{8,9},{10,11},{12,13},{14,15},{1,17},{3,19... | collective-permute-start | bytes 1769480 | tf_op jit(solution)/shard_map/ppermute | solution.py:33
  8.4 1.5 %collective-permute-start.1 = (bf16[384,768]{1,0:T(8,128)(2,1)}, bf16[384,768]{1,0:T(8,128)(2,1)}, u32[]{:S(2)}, u32[]{:S(2)}) collective-permute-start(bf16[384,768]{1,0:T(8,128)(2,1)} %shard_map.73.own_ref), channel_id=1, source_target_pairs={{1,16},{3,18},{5,20},{7,22},{9,24},{11,26},{13,28},{15,30},{16,1},... | collective-permute-start | bytes 1769480 | tf_op jit(solution)/shard_map/ppermute | solution.py:33
  9.9 0.1 stack.80.info
  10.0 0.0 copy-start
  10.0 2.3 %copy-done = bf16[1,1500,1500]{2,1,0:T(8,128)(2,1)S(1)} copy-done((bf16[1,1500,1500]{2,1,0:T(8,128)(2,1)S(1)}, bf16[1,1500,1500]{2,1,0:T(8,128)(2,1)}, u32[]{:S(2)}) %copy-start) | copy-done | bytes 4500024
  12.3 2.9 %shard_map.75 = (bf16[384,1536]{1,0:T(8,128)(2,1)S(1)}, bf16[2,8,96,384]{3,2,1,0:T(8,128)(2,1)S(1)}) custom-call(s32[16]{0:T(128)S(1)} %stack.80.info, bf16[1536,384]{1,0:T(8,128)(2,1)S(1)} %get-tuple-element.52.x_ref, bf16[1,1500,1500]{2,1,0:T(8,128)(2,1)S(1)} %copy-done), custom_call_target="tpu_custom_call" | custom-call | flops 1 | bytes 1 | tf_op jit(solution)/shard_map/pallas_call | solution.py:53
  15.1 8.6 %collective-permute-done.a_ref = bf16[384,768]{1,0:T(8,128)(2,1)} collective-permute-done((bf16[384,768]{1,0:T(8,128)(2,1)}, bf16[384,768]{1,0:T(8,128)(2,1)}, u32[]{:S(2)}, u32[]{:S(2)}) %collective-permute-start) | collective-permute-done | bytes 589856 | tf_op jit(solution)/shard_map/ppermute | solution.py:33
  23.8 0.0 collective-permute-done.1.b_ref
  23.8 2.8 %collective-permute-start.5 = (bf16[1536,384]{1,0:T(8,128)(2,1)S(1)}, bf16[1536,384]{1,0:T(8,128)(2,1)S(1)}, u32[]{:S(2)}, u32[]{:S(2)}) collective-permute-start(bf16[1536,384]{1,0:T(8,128)(2,1)S(1)} %get-tuple-element.52.x_ref), channel_id=1, source_target_pairs={{0,17},{2,19},{4,21},{6,23},{8,25},{10,27},{12,29},{14,31},{1,16},... | collective-permute-start | bytes 3538952 | tf_op jit(solution)/shard_map/ppermute | solution.py:33
  26.6 1.5 %shard_map.76.refs_5_ = bf16[2,384,768]{2,1,0:T(8,128)(2,1)S(1)} custom-call(s32[16]{0:T(128)S(1)} %stack.80.info, bf16[384,768]{1,0:T(8,128)(2,1)} %shard_map.73.own_ref, bf16[384,768]{1,0:T(8,128)(2,1)} %collective-permute-done.a_ref, bf16[384,768]{1,0:T(8,128)(2,1)} %collective-permute-done.1.b_ref), custom_call_target="tpu_custom_call" | custom-call | flops 8000000000 | bytes 8000001 | tf_op jit(solution)/shard_map/pallas_call | solution.py:53
  28.1 1.6 %collective-permute-start.3 = (bf16[2,384,768]{2,1,0:T(8,128)(2,1)S(1)}, bf16[2,384,768]{2,1,0:T(8,128)(2,1)S(1)}, u32[]{:S(2)}, u32[]{:S(2)}) collective-permute-start(bf16[2,384,768]{2,1,0:T(8,128)(2,1)S(1)} %shard_map.76.refs_5_), channel_id=1, source_target_pairs={{0,2},{2,4},{4,6},{6,0},{8,10},{10,12},{12,14},{14,8},{1,3},{3,5},... | collective-permute-start | bytes 3538952 | tf_op jit(solution)/shard_map/ppermute | solution.py:33
  29.8 1.7 %collective-permute-start.4 = (bf16[2,384,768]{2,1,0:T(8,128)(2,1)S(1)}, bf16[2,384,768]{2,1,0:T(8,128)(2,1)S(1)}, u32[]{:S(2)}, u32[]{:S(2)}) collective-permute-start(bf16[2,384,768]{2,1,0:T(8,128)(2,1)S(1)} %shard_map.76.refs_5_), channel_id=1, source_target_pairs={{0,6},{2,0},{4,2},{6,4},{8,14},{10,8},{12,10},{14,12},{1,7},{3,1},... | collective-permute-start | bytes 3538952 | tf_op jit(solution)/shard_map/ppermute | solution.py:33
  31.4 4.6 %collective-permute-done.6.refs_1_ = bf16[2,1536,384]{2,1,0:T(8,128)(2,1)S(1)} collective-permute-done((bf16[2,1536,384]{2,1,0:T(8,128)(2,1)}, bf16[2,1536,384]{2,1,0:T(8,128)(2,1)S(1)}, u32[]{:S(2)}, u32[]{:S(2)}) %collective-permute-start.6) | collective-permute-done | bytes 2359328 | tf_op jit(solution)/shard_map/ppermute | solution.py:33
  36.0 0.1 slice_bitcast_fusion
  36.2 0.1 collective-permute-start.8
  36.3 2.3 %collective-permute-start.7 = (bf16[2,1536,384]{2,1,0:T(8,128)(2,1)S(1)}, bf16[2,1536,384]{2,1,0:T(8,128)(2,1)S(1)}, u32[]{:S(2)}, u32[]{:S(2)}) collective-permute-start(bf16[2,1536,384]{2,1,0:T(8,128)(2,1)S(1)} %collective-permute-done.6.refs_1_), channel_id=1, source_target_pairs={{0,8},{2,10},{4,12},{6,14},{8,0},{10,2},{12,4},{14,6},{1,9},{3,11}... | collective-permute-start | bytes 7077896 | tf_op jit(solution)/shard_map/ppermute | solution.py:33
  38.6 0.3 shard_map.77.amp_ref
  38.9 15.0 %collective-permute-done.5.x_ref = bf16[1536,384]{1,0:T(8,128)(2,1)S(1)} collective-permute-done((bf16[1536,384]{1,0:T(8,128)(2,1)S(1)}, bf16[1536,384]{1,0:T(8,128)(2,1)S(1)}, u32[]{:S(2)}, u32[]{:S(2)}) %collective-permute-start.5) | collective-permute-done | bytes 1179680 | tf_op jit(solution)/shard_map/ppermute | solution.py:33
  53.9 2.9 %shard_map.78 = (bf16[384,1536]{1,0:T(8,128)(2,1)S(1)}, bf16[2,8,96,384]{3,2,1,0:T(8,128)(2,1)S(1)}) custom-call(s32[16]{0:T(128)S(1)} %stack.80.info, bf16[1536,384]{1,0:T(8,128)(2,1)S(1)} %collective-permute-done.5.x_ref, bf16[1,1500,1500]{2,1,0:T(8,128)(2,1)S(1)} %shard_map.77.amp_ref), custom_call_target="tpu_custom_call" | custom-call | flops 10000000000 | bytes 10000001 | tf_op jit(solution)/shard_map/pallas_call | solution.py:53
  56.8 1.3 %collective-permute-done.3.first_ref.refs_7_ = bf16[2,384,768]{2,1,0:T(8,128)(2,1)S(1)} collective-permute-done((bf16[2,384,768]{2,1,0:T(8,128)(2,1)S(1)}, bf16[2,384,768]{2,1,0:T(8,128)(2,1)S(1)}, u32[]{:S(2)}, u32[]{:S(2)}) %collective-permute-start.3) | collective-permute-done | bytes 1179680 | tf_op jit(solution)/shard_map/ppermute | solution.py:33
  58.0 0.0 collective-permute-done.4.second_ref.refs_6_
  58.1 0.0 collective-permute-done.8.refs_3_
  58.1 0.0 collective-permute-start.9
  58.1 0.6 shard_map.79
  58.7 1.6 %collective-permute-start.10 = (bf16[2,384,768]{2,1,0:T(8,128)(2,1)S(1)}, bf16[2,384,768]{2,1,0:T(8,128)(2,1)S(1)}, u32[]{:S(2)}, u32[]{:S(2)}) collective-permute-start(bf16[2,384,768]{2,1,0:T(8,128)(2,1)S(1)} %shard_map.79), channel_id=1, source_target_pairs={{0,2},{2,4},{4,6},{6,0},{8,14},{10,8},{12,10},{14,12},{1,3},{3,5},... | collective-permute-start | bytes 3538952 | tf_op jit(solution)/shard_map/ppermute | solution.py:33
  60.4 0.6 collective-permute-done.9.refs_4_
  60.9 0.0 collective-permute-done.7.refs_2_
  60.9 15.4 %shard_map.80.refs_6_.early_ref = f32[768,1536]{1,0:T(8,128)S(1)} custom-call(s32[16]{0:T(128)S(1)} %stack.80.info, bf16[384,1536]{1,0:T(8,128)(2,1)S(1)} %get-tuple-element.48.h0_ref, bf16[384,1536]{1,0:T(8,128)(2,1)S(1)} %get-tuple-element.58.h1_ref, bf16[2,1536,384]{2,1,0:T(8,128)(2,1)} %get-tuple-element.53.refs_0_, ...), custom_call_target="tpu_custom_call" | custom-call | flops 1 | bytes 1 | tf_op jit(solution)/shard_map/pallas_call | solution.py:53
  76.4 5.6 %shard_map.81 = (bf16[768,768]{1,0:T(8,128)(2,1)S(1)}, bf16[1536,768]{1,0:T(8,128)(2,1)S(1)}, bf16[768,768]{1,0:T(8,128)(2,1)S(1)}, bf16[768,768]{1,0:T(8,128)(2,1)S(1)}) custom-call(s32[16]{0:T(128)S(1)} %stack.80.info, bf16[384,1536]{1,0:T(8,128)(2,1)S(1)} %get-tuple-element.48.h0_ref, bf16[384,1536]{1,0:T(8,128)(2,1)S(1)} %get-tuple-element.58.h1_ref, ...), custom_call_target="tpu_custom_call" | custom-call | flops 1 | bytes 1 | tf_op jit(solution)/shard_map/pallas_call | solution.py:53
  82.0 1.2 collective-permute-start.11
  83.1 2.9 %shard_map.84 = (bf16[768,768]{1,0:T(8,128)(2,1)S(1)}, bf16[768,768]{1,0:T(8,128)(2,1)S(1)}) custom-call(f32[768,1536]{1,0:T(8,128)S(1)} %shard_map.80.refs_6_.early_ref, bf16[768,768]{1,0:T(8,128)(2,1)S(1)} %get-tuple-element.68.newest_ref, bf16[1536,768]{1,0:T(8,128)(2,1)S(1)} %get-tuple-element.69.xn_ref, ...), custom_call_target="tpu_custom_call" | custom-call | flops 1 | bytes 1 | tf_op jit(solution)/shard_map/pallas_call | solution.py:53
  86.1 0.3 collective-permute-start.13
  86.4 1.2 %shard_map.82 = (f32[384,768]{1,0:T(8,128)S(1)}, bf16[384,768]{1,0:T(8,128)(2,1)S(1)}) custom-call(bf16[768,768]{1,0:T(8,128)(2,1)S(1)} %get-tuple-element.63.back_ref, bf16[2,8,96,384]{3,2,1,0:T(8,128)(2,1)S(1)} %get-tuple-element.61.refs_7_.w0_ref, bf16[2,8,96,384]{3,2,1,0:T(8,128)(2,1)S(1)} %get-tuple-element.62.refs_8_.w1_ref, ...), custom_call_target="tpu_custom_call" | custom-call | flops 1 | bytes 1 | tf_op jit(solution)/shard_map/pallas_call | solution.py:53
  87.6 3.5 %collective-permute-start.12 = (bf16[384,768]{1,0:T(8,128)(2,1)S(1)}, bf16[384,768]{1,0:T(8,128)(2,1)S(1)}, u32[]{:S(2)}, u32[]{:S(2)}) collective-permute-start(bf16[384,768]{1,0:T(8,128)(2,1)S(1)} %get-tuple-element.66), channel_id=1, source_target_pairs={{0,16},{2,18},{4,20},{6,22},{8,24},{10,26},{12,28},{14,30},{1,17},... | collective-permute-start | bytes 1769480 | tf_op jit(solution)/shard_map/ppermute | solution.py:33
  91.1 0.0 collective-permute-done.13.got_ref
  91.2 1.2 %shard_map.85 = (f32[2,96,768]{2,1,0:T(8,128)S(1)}, bf16[2,96,768]{2,1,0:T(8,128)(2,1)S(1)}, bf16[2,96,768]{2,1,0:T(8,128)(2,1)S(1)}, bf16[2,96,768]{2,1,0:T(8,128)(2,1)S(1)}) custom-call(bf16[768,768]{1,0:T(8,128)(2,1)S(1)} %get-tuple-element.70.back_ref, bf16[2,8,96,384]{3,2,1,0:T(8,128)(2,1)S(1)} %get-tuple-element.61.refs_7_.w0_ref, ...), custom_call_target="tpu_custom_call" | custom-call | flops 1 | bytes 1 | tf_op jit(solution)/shard_map/pallas_call | solution.py:53
  92.4 0.0 copy-start.3
  92.4 0.1 collective-permute-start.14
  92.5 1.5 %collective-permute-start.15 = (bf16[2,96,768]{2,1,0:T(8,128)(2,1)S(1)}, bf16[2,96,768]{2,1,0:T(8,128)(2,1)S(1)}, u32[]{:S(2)}, u32[]{:S(2)}) collective-permute-start(bf16[2,96,768]{2,1,0:T(8,128)(2,1)S(1)} %get-tuple-element.73), channel_id=1, source_target_pairs={{0,32},{2,34},{4,36},{6,38},{8,40},{10,42},{12,44},{14,46},{1,33},... | collective-permute-start | bytes 884744 | tf_op jit(solution)/shard_map/ppermute | solution.py:33
  94.1 1.7 %collective-permute-start.16 = (bf16[2,96,768]{2,1,0:T(8,128)(2,1)S(1)}, bf16[2,96,768]{2,1,0:T(8,128)(2,1)S(1)}, u32[]{:S(2)}, u32[]{:S(2)}) collective-permute-start(bf16[2,96,768]{2,1,0:T(8,128)(2,1)S(1)} %get-tuple-element.74), channel_id=1, source_target_pairs={{0,96},{2,98},{4,100},{6,102},{8,104},{10,106},{12,108},{14,110},{... | collective-permute-start | bytes 884744 | tf_op jit(solution)/shard_map/ppermute | solution.py:33
  95.8 9.3 %collective-permute-done.12.got_ref = bf16[384,768]{1,0:T(8,128)(2,1)S(1)} collective-permute-done((bf16[384,768]{1,0:T(8,128)(2,1)S(1)}, bf16[384,768]{1,0:T(8,128)(2,1)S(1)}, u32[]{:S(2)}, u32[]{:S(2)}) %collective-permute-start.12) | collective-permute-done | bytes 589856 | tf_op jit(solution)/shard_map/ppermute | solution.py:33
  105.1 0.1 shard_map.83
  105.2 0.5 collective-permute-start.17
  105.7 1.5 %collective-permute-start.18 = (bf16[96,768]{1,0:T(8,128)(2,1)S(1)}, bf16[96,768]{1,0:T(8,128)(2,1)S(1)}, u32[]{:S(2)}, u32[]{:S(2)}) collective-permute-start(bf16[96,768]{1,0:T(8,128)(2,1)S(1)} %get-tuple-element.77), channel_id=1, source_target_pairs={{0,32},{2,34},{4,36},{6,38},{8,40},{10,42},{12,44},{14,46},{1,33},... | collective-permute-start | bytes 442376 | tf_op jit(solution)/shard_map/ppermute | solution.py:33
  107.3 0.0 collective-permute-done.14.got_1
  107.3 1.7 %collective-permute-start.19 = (bf16[96,768]{1,0:T(8,128)(2,1)S(1)}, bf16[96,768]{1,0:T(8,128)(2,1)S(1)}, u32[]{:S(2)}, u32[]{:S(2)}) collective-permute-start(bf16[96,768]{1,0:T(8,128)(2,1)S(1)} %get-tuple-element.78), channel_id=1, source_target_pairs={{0,96},{2,98},{4,100},{6,102},{8,104},{10,106},{12,108},{14,110},{... | collective-permute-start | bytes 442376 | tf_op jit(solution)/shard_map/ppermute | solution.py:33
  109.7 0.1 pad_add_fusion.numbers
  109.7 0.0 collective-permute-done.15.got_2
  109.7 0.0 collective-permute-done.16.got_3
  109.7 0.1 shard_map.87
  109.9 0.0 copy-start.2
  109.9 3.0 %collective-permute-start.20 = (bf16[96,768]{1,0:T(8,128)(2,1)S(1)}, bf16[96,768]{1,0:T(8,128)(2,1)S(1)}, u32[]{:S(2)}, u32[]{:S(2)}) collective-permute-start(bf16[96,768]{1,0:T(8,128)(2,1)S(1)} %get-tuple-element.84), channel_id=1, source_target_pairs={{0,16},{2,18},{4,20},{6,22},{8,24},{10,26},{12,28},{14,30},{1,17},... | collective-permute-start | bytes 442376 | tf_op jit(solution)/shard_map/ppermute | solution.py:33
  112.9 0.7 collective-permute-done.17.refs_0_
  113.6 1.9 %collective-permute-done.18.refs_1_ = bf16[96,768]{1,0:T(8,128)(2,1)S(1)} collective-permute-done((bf16[96,768]{1,0:T(8,128)(2,1)S(1)}, bf16[96,768]{1,0:T(8,128)(2,1)S(1)}, u32[]{:S(2)}, u32[]{:S(2)}) %collective-permute-start.18) | collective-permute-done | bytes 147488 | tf_op jit(solution)/shard_map/ppermute | solution.py:33
  115.5 0.1 shard_map.86.a_ref
  115.6 1.0 collective-permute-done.20.b1_ref
  116.6 0.9 shard_map.88
  117.5 0.9 reshape.11
  118.5 0.8 slice.9
  (13 shorter events, 0.0 us)
Async XLA Ops:
  0.0 3.0 %copy-start.1 = (bf16[1500,375]{1,0:T(8,128)(2,1)S(1)}, bf16[1500,375]{1,0:T(8,128)(2,1)}, u32[]{:S(2)}) copy-start(bf16[1500,375]{1,0:T(8,128)(2,1)} %own_ref.1) | copy-start | bytes 3375004
  0.0 3.0 %collective-permute-start.2 = (bf16[1500,375]{1,0:T(8,128)(2,1)}, bf16[1500,375]{1,0:T(8,128)(2,1)S(1)}, u32[]{:S(2)}, u32[]{:S(2)}) collective-permute-start(bf16[1500,375]{1,0:T(8,128)(2,1)} %own_ref.1), channel_id=1, source_target_pairs={{0,8},{2,10},{4,12},{6,14},{8,0},{10,2},{12,4},{14,6},{1,9},{3,11}... | collective-permute-start | bytes 3375008 | tf_op jit(solution)/shard_map/ppermute | solution.py:33
  4.9 31.2 %collective-permute-start.6 = (bf16[2,1536,384]{2,1,0:T(8,128)(2,1)}, bf16[2,1536,384]{2,1,0:T(8,128)(2,1)S(1)}, u32[]{:S(2)}, u32[]{:S(2)}) collective-permute-start(bf16[2,1536,384]{2,1,0:T(8,128)(2,1)} %get-tuple-element.53.refs_0_), channel_id=1, source_target_pairs={{0,32},{2,34},{4,36},{6,38},{8,104},{10,106},{12,108},{14,110},{1,... | collective-permute-start | bytes 7077896 | tf_op jit(solution)/shard_map/ppermute | solution.py:33
  6.9 16.9 %collective-permute-start = (bf16[384,768]{1,0:T(8,128)(2,1)}, bf16[384,768]{1,0:T(8,128)(2,1)}, u32[]{:S(2)}, u32[]{:S(2)}) collective-permute-start(bf16[384,768]{1,0:T(8,128)(2,1)} %shard_map.73.own_ref), channel_id=1, source_target_pairs={{0,1},{2,3},{4,5},{6,7},{8,9},{10,11},{12,13},{14,15},{1,17},{3,19... | collective-permute-start | bytes 1769480 | tf_op jit(solution)/shard_map/ppermute | solution.py:33
  8.4 15.4 %collective-permute-start.1 = (bf16[384,768]{1,0:T(8,128)(2,1)}, bf16[384,768]{1,0:T(8,128)(2,1)}, u32[]{:S(2)}, u32[]{:S(2)}) collective-permute-start(bf16[384,768]{1,0:T(8,128)(2,1)} %shard_map.73.own_ref), channel_id=1, source_target_pairs={{1,16},{3,18},{5,20},{7,22},{9,24},{11,26},{13,28},{15,30},{16,1},... | collective-permute-start | bytes 1769480 | tf_op jit(solution)/shard_map/ppermute | solution.py:33
  10.0 2.3 %copy-start = (bf16[1,1500,1500]{2,1,0:T(8,128)(2,1)S(1)}, bf16[1,1500,1500]{2,1,0:T(8,128)(2,1)}, u32[]{:S(2)}) copy-start(bf16[1,1500,1500]{2,1,0:T(8,128)(2,1)} %in_ref) | copy-start | bytes 13500004
  23.8 14.8 %slice-start = ((s8[4620288]{0:T(1024)(128)(4,1)}), s8[4194304]{0:T(1024)(128)(4,1)S(1)}, s32[]{:S(2)}) async-start(s8[4620288]{0:T(1024)(128)(4,1)} %bitcast.20), calls=%async_computation | async-start | bytes 8388608
  23.8 14.8 %slice-start.1 = ((s8[4620288]{0:T(1024)(128)(4,1)}), s8[425984]{0:T(1024)(128)(4,1)S(1)}, s32[]{:S(2)}) async-start(s8[4620288]{0:T(1024)(128)(4,1)} %bitcast.20), calls=%async_computation.1 | async-start | bytes 851968
  23.8 30.1 %collective-permute-start.5 = (bf16[1536,384]{1,0:T(8,128)(2,1)S(1)}, bf16[1536,384]{1,0:T(8,128)(2,1)S(1)}, u32[]{:S(2)}, u32[]{:S(2)}) collective-permute-start(bf16[1536,384]{1,0:T(8,128)(2,1)S(1)} %get-tuple-element.52.x_ref), channel_id=1, source_target_pairs={{0,17},{2,19},{4,21},{6,23},{8,25},{10,27},{12,29},{14,31},{1,16},... | collective-permute-start | bytes 3538952 | tf_op jit(solution)/shard_map/ppermute | solution.py:33
  28.1 29.9 %collective-permute-start.3 = (bf16[2,384,768]{2,1,0:T(8,128)(2,1)S(1)}, bf16[2,384,768]{2,1,0:T(8,128)(2,1)S(1)}, u32[]{:S(2)}, u32[]{:S(2)}) collective-permute-start(bf16[2,384,768]{2,1,0:T(8,128)(2,1)S(1)} %shard_map.76.refs_5_), channel_id=1, source_target_pairs={{0,2},{2,4},{4,6},{6,0},{8,10},{10,12},{12,14},{14,8},{1,3},{3,5},... | collective-permute-start | bytes 3538952 | tf_op jit(solution)/shard_map/ppermute | solution.py:33
  29.8 28.3 %collective-permute-start.4 = (bf16[2,384,768]{2,1,0:T(8,128)(2,1)S(1)}, bf16[2,384,768]{2,1,0:T(8,128)(2,1)S(1)}, u32[]{:S(2)}, u32[]{:S(2)}) collective-permute-start(bf16[2,384,768]{2,1,0:T(8,128)(2,1)S(1)} %shard_map.76.refs_5_), channel_id=1, source_target_pairs={{0,6},{2,0},{4,2},{6,4},{8,14},{10,8},{12,10},{14,12},{1,7},{3,1},... | collective-permute-start | bytes 3538952 | tf_op jit(solution)/shard_map/ppermute | solution.py:33
  36.2 21.9 %collective-permute-start.8 = (bf16[1536,384]{1,0:T(8,128)(2,1)S(1)}, bf16[1536,384]{1,0:T(8,128)(2,1)S(1)}, u32[]{:S(2)}, u32[]{:S(2)}) collective-permute-start(bf16[1536,384]{1,0:T(8,128)(2,1)S(1)} %slice_bitcast_fusion), channel_id=1, source_target_pairs={{0,32},{2,34},{4,36},{6,38},{8,104},{10,106},{12,108},{14,110},{1,... | collective-permute-start | bytes 3538952 | tf_op jit(solution)/shard_map/ppermute | solution.py:33
  36.3 24.7 %collective-permute-start.7 = (bf16[2,1536,384]{2,1,0:T(8,128)(2,1)S(1)}, bf16[2,1536,384]{2,1,0:T(8,128)(2,1)S(1)}, u32[]{:S(2)}, u32[]{:S(2)}) collective-permute-start(bf16[2,1536,384]{2,1,0:T(8,128)(2,1)S(1)} %collective-permute-done.6.refs_1_), channel_id=1, source_target_pairs={{0,8},{2,10},{4,12},{6,14},{8,0},{10,2},{12,4},{14,6},{1,9},{3,11}... | collective-permute-start | bytes 7077896 | tf_op jit(solution)/shard_map/ppermute | solution.py:33
  58.1 2.8 %collective-permute-start.9 = (bf16[1536,384]{1,0:T(8,128)(2,1)S(1)}, bf16[1536,384]{1,0:T(8,128)(2,1)S(1)}, u32[]{:S(2)}, u32[]{:S(2)}) collective-permute-start(bf16[1536,384]{1,0:T(8,128)(2,1)S(1)} %collective-permute-done.8.refs_3_), channel_id=1, source_target_pairs={{0,8},{2,10},{4,12},{6,14},{8,0},{10,2},{12,4},{14,6},{1,9},{3,11}... | collective-permute-start | bytes 3538952 | tf_op jit(solution)/shard_map/ppermute | solution.py:33
  58.7 17.6 %collective-permute-start.10 = (bf16[2,384,768]{2,1,0:T(8,128)(2,1)S(1)}, bf16[2,384,768]{2,1,0:T(8,128)(2,1)S(1)}, u32[]{:S(2)}, u32[]{:S(2)}) collective-permute-start(bf16[2,384,768]{2,1,0:T(8,128)(2,1)S(1)} %shard_map.79), channel_id=1, source_target_pairs={{0,2},{2,4},{4,6},{6,0},{8,14},{10,8},{12,10},{14,12},{1,3},{3,5},... | collective-permute-start | bytes 3538952 | tf_op jit(solution)/shard_map/ppermute | solution.py:33
  82.0 4.4 %collective-permute-start.11 = (bf16[768,768]{1,0:T(8,128)(2,1)S(1)}, bf16[768,768]{1,0:T(8,128)(2,1)S(1)}, u32[]{:S(2)}, u32[]{:S(2)}) collective-permute-start(bf16[768,768]{1,0:T(8,128)(2,1)S(1)} %get-tuple-element.64), channel_id=1, source_target_pairs={{0,8},{2,10},{4,12},{6,14},{8,0},{10,2},{12,4},{14,6},{1,9},{3,11}... | collective-permute-start | bytes 3538952 | tf_op jit(solution)/shard_map/ppermute | solution.py:33
  86.1 5.1 %collective-permute-start.13 = (bf16[768,768]{1,0:T(8,128)(2,1)S(1)}, bf16[768,768]{1,0:T(8,128)(2,1)S(1)}, u32[]{:S(2)}, u32[]{:S(2)}) collective-permute-start(bf16[768,768]{1,0:T(8,128)(2,1)S(1)} %get-tuple-element.71), channel_id=1, source_target_pairs={{0,8},{2,10},{4,12},{6,14},{8,0},{10,2},{12,4},{14,6},{1,9},{3,11}... | collective-permute-start | bytes 3538952 | tf_op jit(solution)/shard_map/ppermute | solution.py:33
  87.6 17.5 %collective-permute-start.12 = (bf16[384,768]{1,0:T(8,128)(2,1)S(1)}, bf16[384,768]{1,0:T(8,128)(2,1)S(1)}, u32[]{:S(2)}, u32[]{:S(2)}) collective-permute-start(bf16[384,768]{1,0:T(8,128)(2,1)S(1)} %get-tuple-element.66), channel_id=1, source_target_pairs={{0,16},{2,18},{4,20},{6,22},{8,24},{10,26},{12,28},{14,30},{1,17},... | collective-permute-start | bytes 1769480 | tf_op jit(solution)/shard_map/ppermute | solution.py:33
  92.4 17.2 %copy-start.3 = (f32[1500]{0:T(1024)S(1)}, f32[1500]{0:T(1024)}, u32[]{:S(2)}) copy-start(f32[1500]{0:T(1024)} %param.12) | copy-start | bytes 18004
  92.4 14.9 %collective-permute-start.14 = (bf16[2,96,768]{2,1,0:T(8,128)(2,1)S(1)}, bf16[2,96,768]{2,1,0:T(8,128)(2,1)S(1)}, u32[]{:S(2)}, u32[]{:S(2)}) collective-permute-start(bf16[2,96,768]{2,1,0:T(8,128)(2,1)S(1)} %get-tuple-element.72), channel_id=1, source_target_pairs={{0,64},{2,66},{4,68},{6,70},{8,72},{10,74},{12,76},{14,78},{1,65},... | collective-permute-start | bytes 884744 | tf_op jit(solution)/shard_map/ppermute | solution.py:33
  92.5 17.2 %collective-permute-start.15 = (bf16[2,96,768]{2,1,0:T(8,128)(2,1)S(1)}, bf16[2,96,768]{2,1,0:T(8,128)(2,1)S(1)}, u32[]{:S(2)}, u32[]{:S(2)}) collective-permute-start(bf16[2,96,768]{2,1,0:T(8,128)(2,1)S(1)} %get-tuple-element.73), channel_id=1, source_target_pairs={{0,32},{2,34},{4,36},{6,38},{8,40},{10,42},{12,44},{14,46},{1,33},... | collective-permute-start | bytes 884744 | tf_op jit(solution)/shard_map/ppermute | solution.py:33
  94.1 15.7 %collective-permute-start.16 = (bf16[2,96,768]{2,1,0:T(8,128)(2,1)S(1)}, bf16[2,96,768]{2,1,0:T(8,128)(2,1)S(1)}, u32[]{:S(2)}, u32[]{:S(2)}) collective-permute-start(bf16[2,96,768]{2,1,0:T(8,128)(2,1)S(1)} %get-tuple-element.74), channel_id=1, source_target_pairs={{0,96},{2,98},{4,100},{6,102},{8,104},{10,106},{12,108},{14,110},{... | collective-permute-start | bytes 884744 | tf_op jit(solution)/shard_map/ppermute | solution.py:33
  105.2 8.4 %collective-permute-start.17 = (bf16[96,768]{1,0:T(8,128)(2,1)S(1)}, bf16[96,768]{1,0:T(8,128)(2,1)S(1)}, u32[]{:S(2)}, u32[]{:S(2)}) collective-permute-start(bf16[96,768]{1,0:T(8,128)(2,1)S(1)} %get-tuple-element.76), channel_id=1, source_target_pairs={{0,64},{2,66},{4,68},{6,70},{8,72},{10,74},{12,76},{14,78},{1,65},... | collective-permute-start | bytes 442376 | tf_op jit(solution)/shard_map/ppermute | solution.py:33
  105.7 9.8 %collective-permute-start.18 = (bf16[96,768]{1,0:T(8,128)(2,1)S(1)}, bf16[96,768]{1,0:T(8,128)(2,1)S(1)}, u32[]{:S(2)}, u32[]{:S(2)}) collective-permute-start(bf16[96,768]{1,0:T(8,128)(2,1)S(1)} %get-tuple-element.77), channel_id=1, source_target_pairs={{0,32},{2,34},{4,36},{6,38},{8,40},{10,42},{12,44},{14,46},{1,33},... | collective-permute-start | bytes 442376 | tf_op jit(solution)/shard_map/ppermute | solution.py:33
  107.3 8.3 %collective-permute-start.19 = (bf16[96,768]{1,0:T(8,128)(2,1)S(1)}, bf16[96,768]{1,0:T(8,128)(2,1)S(1)}, u32[]{:S(2)}, u32[]{:S(2)}) collective-permute-start(bf16[96,768]{1,0:T(8,128)(2,1)S(1)} %get-tuple-element.78), channel_id=1, source_target_pairs={{0,96},{2,98},{4,100},{6,102},{8,104},{10,106},{12,108},{14,110},{... | collective-permute-start | bytes 442376 | tf_op jit(solution)/shard_map/ppermute | solution.py:33
  109.9 6.7 %copy-start.2 = (f32[150]{0:T(256)S(1)}, f32[150]{0:T(256)}, u32[]{:S(2)}) copy-start(f32[150]{0:T(256)} %param.13) | copy-start | bytes 1804
  109.9 6.7 %collective-permute-start.20 = (bf16[96,768]{1,0:T(8,128)(2,1)S(1)}, bf16[96,768]{1,0:T(8,128)(2,1)S(1)}, u32[]{:S(2)}, u32[]{:S(2)}) collective-permute-start(bf16[96,768]{1,0:T(8,128)(2,1)S(1)} %get-tuple-element.84), channel_id=1, source_target_pairs={{0,16},{2,18},{4,20},{6,22},{8,24},{10,26},{12,28},{14,30},{1,17},... | collective-permute-start | bytes 442376 | tf_op jit(solution)/shard_map/ppermute | solution.py:33

commit v3 on v2

--- a/solution.py
+++ b/solution.py
@@ -214,16 +214,19 @@
 
 def last_block(info, h0_ref, h1_ref, *refs):
     x_refs, z_ref, early_ref, w0_ref, w1_ref = refs[:5], *refs[5:9]
-    w_out, xn_out, back_out, give_ref, left, xsem, vsem = refs[9:]
+    w_out, xn_out, back_out, give_ref, keep_ref, left, xsem, vsem, ksem = refs[9:]
     newest = Factors(info, 3, x_refs, xn_out, 0, xsem)
     newest.start()
     left_loads = window_loads(0, w0_ref, w1_ref, left, vsem)
+    keep_loads = window_loads(1, w0_ref, w1_ref, keep_ref, ksem)
     newest.wait()
     for b, h_ref in enumerate((h0_ref, h1_ref)):
         w_out[b * BPAD : b * BPAD + BPAD, :] = weigh(h_ref, xn_out[...], z_ref[b])
     part = dot(w_out[...], xn_out[:TWO, :], 1, 1)
     back_out[...] = (early_ref[:, :TWO] + part).astype(BF16)
     give_half(left_loads, left, back_out[...], give_ref)
+    for load in keep_loads:
+        load.wait()
 
 
 def second_half(early_ref, newest_ref, xn_ref, w0_ref, w1_ref, back_out, give_ref, left, vsem):
@@ -233,21 +236,19 @@
     give_half(left_loads, left, back_out[...], give_ref)
 
 
-def keep_sum(back_ref, w0_ref, w1_ref, got_ref, left, vsem):
-    for load in window_loads(1, w0_ref, w1_ref, left, vsem):
-        load.wait()
-    return dot(left[...].reshape(8 * WIN, TWO), back_ref[...], 1, 0) + got_ref[...].astype(F32)
-
-
-def keep_x(back_ref, w0_ref, w1_ref, got_ref, own_ref, send_ref, left, vsem):
-    total = keep_sum(back_ref, w0_ref, w1_ref, got_ref, left, vsem)
+def keep_sum(back_ref, left_ref, got_ref):
+    left = left_ref[...].reshape(8 * WIN, TWO)
+    return dot(left, back_ref[...], 1, 0) + got_ref[...].astype(F32)
+
+
+def keep_x(back_ref, left_ref, got_ref, own_ref, send_ref):
+    total = keep_sum(back_ref, left_ref, got_ref)
     own_ref[...] = total[: 4 * WIN]
     send_ref[...] = total[4 * WIN :].astype(BF16)
 
 
-def keep_z(back_ref, w0_ref, w1_ref, got_ref, own_ref, *refs):
-    send_refs, left, vsem = refs[:3], refs[3], refs[4]
-    total = keep_sum(back_ref, w0_ref, w1_ref, got_ref, left, vsem)
+def keep_z(back_ref, left_ref, got_ref, own_ref, *send_refs):
+    total = keep_sum(back_ref, left_ref, got_ref)
     for dx in range(2):
         for dz in range(4):
             part = total[(4 * dx + dz) * WIN : (4 * dx + dz + 1) * WIN]
@@ -417,10 +418,10 @@
     )
     left = pltpu.VMEM((8, WIN, TWO), BF16)
     half_shape = shape(TWO, TWO)
-    newest, x_newest, back_a, give_a = call(
+    newest, x_newest, back_a, give_a, kept = call(
         last_block,
-        (half_shape, shape(VPAD, TWO), half_shape, half_shape),
-        [left, dma((2,)), dma((2,))],
+        (half_shape, shape(VPAD, TWO), half_shape, half_shape, shape(8, WIN, TWO)),
+        [left, dma((2,)), dma((2,)), dma((2,))],
         info,
         half_0,
         half_1,
@@ -450,23 +451,19 @@
     own_a, send_a = call(
         keep_x,
         (shape(4 * WIN, TWO, dtype=F32), shape(4 * WIN, TWO)),
-        [left, dma((2,))],
+        [],
         back_a,
-        wins_0,
-        wins_1,
+        kept,
         got_a,
-        in_specs=[VMEM, HBM, HBM, VMEM],
     )
     from_x = move(send_a, to_x)
     own_b, *sends_b = call(
         keep_z,
         tuple([shape(2, WIN, TWO, dtype=F32)] + [shape(2, WIN, TWO)] * 3),
-        [left, dma((2,))],
+        [],
         back_b,
-        wins_0,
-        wins_1,
+        kept,
         got_b,
-        in_specs=[VMEM, HBM, HBM, VMEM],
     )
     from_z = [move(sends_b[dz - 1], to_z[dz]) for dz in (2, 1, 3)]
     total_a, *sends_a = call(

time: 120 us -> 120 us (level)
  no operation moved by 1% of the time
where the time goes in v3:
time: 120 us; the launch traced here: 119 us
  waiting for transfers between devices  43.3 us (36%)
  Pallas kernels  40.4 us (34%)
  starting transfers between devices  30.3 us (25%)
  local copies, waits for them, and re-layouts  4.34 us (4%)
    ppermute x21, waiting for transfers between devices, move(): return lax.ppermute(block, BOTH, pairs)  43.3 us
    pallas_call x16, Pallas kernels, call(): pl.pallas_call(kernel, out_shape=out_shape, in_specs=in_specs or [VMEM] *...  40.4 us
    ppermute x21, starting transfers between devices, move(): return lax.ppermute(block, BOTH, pairs)  30.3 us
  transfers between devices with their start and end apart: 21, of which 10 were waited for; matrix products, arithmetic and copies ran while one was open for 0% of the time, Pallas kernels for 27%

profile of v3, /device:TPU:0, one launch (start us, length us, event | category | flops | bytes accessed | tf_op | source)
XLA Modules:
  0.0 119.2 jit_solution(11488841694751964278)
XLA Ops:
  0.0 0.0 collective-permute-start.2
  0.0 2.9 %shard_map.73.own_ref = bf16[384,768]{1,0:T(8,128)(2,1)} custom-call(bf16[375,750]{1,0:T(8,128)(2,1)} %z_hbm.1, f32[3,6]{1,0:T(4,128)} %s_ref.1), custom_call_target="tpu_custom_call" | custom-call | flops 1 | bytes 1 | tf_op jit(solution)/shard_map/pallas_call | solution.py:53
  2.9 0.1 collective-permute-done.2.pair_ref
  3.0 1.9 %shard_map.74 = (bf16[2,1536,384]{2,1,0:T(8,128)(2,1)}, bf16[1536,384]{1,0:T(8,128)(2,1)S(1)}) custom-call(bf16[1500,375]{1,0:T(8,128)(2,1)S(1)} %copy-done.1, bf16[1500,375]{1,0:T(8,128)(2,1)S(1)} %collective-permute-done.2.pair_ref), custom_call_target="tpu_custom_call" | custom-call | flops 1 | bytes 1 | tf_op jit(solution)/shard_map/pallas_call | solution.py:53
  4.9 2.0 %collective-permute-start.6 = (bf16[2,1536,384]{2,1,0:T(8,128)(2,1)}, bf16[2,1536,384]{2,1,0:T(8,128)(2,1)S(1)}, u32[]{:S(2)}, u32[]{:S(2)}) collective-permute-start(bf16[2,1536,384]{2,1,0:T(8,128)(2,1)} %get-tuple-element.54.refs_0_), channel_id=1, source_target_pairs={{0,32},{2,34},{4,36},{6,38},{8,104},{10,106},{12,108},{14,110},{1,... | collective-permute-start | bytes 7077896 | tf_op jit(solution)/shard_map/ppermute | solution.py:33
  6.9 1.5 %collective-permute-start = (bf16[384,768]{1,0:T(8,128)(2,1)}, bf16[384,768]{1,0:T(8,128)(2,1)}, u32[]{:S(2)}, u32[]{:S(2)}) collective-permute-start(bf16[384,768]{1,0:T(8,128)(2,1)} %shard_map.73.own_ref), channel_id=1, source_target_pairs={{0,1},{2,3},{4,5},{6,7},{8,9},{10,11},{12,13},{14,15},{1,17},{3,19... | collective-permute-start | bytes 1769480 | tf_op jit(solution)/shard_map/ppermute | solution.py:33
  8.4 1.5 %collective-permute-start.1 = (bf16[384,768]{1,0:T(8,128)(2,1)}, bf16[384,768]{1,0:T(8,128)(2,1)}, u32[]{:S(2)}, u32[]{:S(2)}) collective-permute-start(bf16[384,768]{1,0:T(8,128)(2,1)} %shard_map.73.own_ref), channel_id=1, source_target_pairs={{1,16},{3,18},{5,20},{7,22},{9,24},{11,26},{13,28},{15,30},{16,1},... | collective-permute-start | bytes 1769480 | tf_op jit(solution)/shard_map/ppermute | solution.py:33
  9.9 0.1 stack.80.info
  10.0 0.0 copy-start
  10.0 2.3 %copy-done = bf16[1,1500,1500]{2,1,0:T(8,128)(2,1)S(1)} copy-done((bf16[1,1500,1500]{2,1,0:T(8,128)(2,1)S(1)}, bf16[1,1500,1500]{2,1,0:T(8,128)(2,1)}, u32[]{:S(2)}) %copy-start) | copy-done | bytes 4500024
  12.3 2.9 %shard_map.75 = (bf16[384,1536]{1,0:T(8,128)(2,1)S(1)}, bf16[2,8,96,384]{3,2,1,0:T(8,128)(2,1)S(1)}) custom-call(s32[16]{0:T(128)S(1)} %stack.80.info, bf16[1536,384]{1,0:T(8,128)(2,1)S(1)} %get-tuple-element.53.x_ref, bf16[1,1500,1500]{2,1,0:T(8,128)(2,1)S(1)} %copy-done), custom_call_target="tpu_custom_call" | custom-call | flops 1 | bytes 1 | tf_op jit(solution)/shard_map/pallas_call | solution.py:53
  15.1 8.6 %collective-permute-done.a_ref = bf16[384,768]{1,0:T(8,128)(2,1)} collective-permute-done((bf16[384,768]{1,0:T(8,128)(2,1)}, bf16[384,768]{1,0:T(8,128)(2,1)}, u32[]{:S(2)}, u32[]{:S(2)}) %collective-permute-start) | collective-permute-done | bytes 589856 | tf_op jit(solution)/shard_map/ppermute | solution.py:33
  23.8 0.0 collective-permute-done.1.b_ref
  23.8 2.8 %collective-permute-start.5 = (bf16[1536,384]{1,0:T(8,128)(2,1)S(1)}, bf16[1536,384]{1,0:T(8,128)(2,1)S(1)}, u32[]{:S(2)}, u32[]{:S(2)}) collective-permute-start(bf16[1536,384]{1,0:T(8,128)(2,1)S(1)} %get-tuple-element.53.x_ref), channel_id=1, source_target_pairs={{0,17},{2,19},{4,21},{6,23},{8,25},{10,27},{12,29},{14,31},{1,16},... | collective-permute-start | bytes 3538952 | tf_op jit(solution)/shard_map/ppermute | solution.py:33
  26.6 1.5 %shard_map.76.refs_5_ = bf16[2,384,768]{2,1,0:T(8,128)(2,1)S(1)} custom-call(s32[16]{0:T(128)S(1)} %stack.80.info, bf16[384,768]{1,0:T(8,128)(2,1)} %shard_map.73.own_ref, bf16[384,768]{1,0:T(8,128)(2,1)} %collective-permute-done.a_ref, bf16[384,768]{1,0:T(8,128)(2,1)} %collective-permute-done.1.b_ref), custom_call_target="tpu_custom_call" | custom-call | flops 8000000000 | bytes 8000001 | tf_op jit(solution)/shard_map/pallas_call | solution.py:53
  28.1 1.6 %collective-permute-start.3 = (bf16[2,384,768]{2,1,0:T(8,128)(2,1)S(1)}, bf16[2,384,768]{2,1,0:T(8,128)(2,1)S(1)}, u32[]{:S(2)}, u32[]{:S(2)}) collective-permute-start(bf16[2,384,768]{2,1,0:T(8,128)(2,1)S(1)} %shard_map.76.refs_5_), channel_id=1, source_target_pairs={{0,2},{2,4},{4,6},{6,0},{8,10},{10,12},{12,14},{14,8},{1,3},{3,5},... | collective-permute-start | bytes 3538952 | tf_op jit(solution)/shard_map/ppermute | solution.py:33
  29.8 1.7 %collective-permute-start.4 = (bf16[2,384,768]{2,1,0:T(8,128)(2,1)S(1)}, bf16[2,384,768]{2,1,0:T(8,128)(2,1)S(1)}, u32[]{:S(2)}, u32[]{:S(2)}) collective-permute-start(bf16[2,384,768]{2,1,0:T(8,128)(2,1)S(1)} %shard_map.76.refs_5_), channel_id=1, source_target_pairs={{0,6},{2,0},{4,2},{6,4},{8,14},{10,8},{12,10},{14,12},{1,7},{3,1},... | collective-permute-start | bytes 3538952 | tf_op jit(solution)/shard_map/ppermute | solution.py:33
  31.4 4.6 %collective-permute-done.6.refs_1_ = bf16[2,1536,384]{2,1,0:T(8,128)(2,1)S(1)} collective-permute-done((bf16[2,1536,384]{2,1,0:T(8,128)(2,1)}, bf16[2,1536,384]{2,1,0:T(8,128)(2,1)S(1)}, u32[]{:S(2)}, u32[]{:S(2)}) %collective-permute-start.6) | collective-permute-done | bytes 2359328 | tf_op jit(solution)/shard_map/ppermute | solution.py:33
  36.0 0.1 slice_bitcast_fusion
  36.2 0.1 collective-permute-start.8
  36.3 2.3 %collective-permute-start.7 = (bf16[2,1536,384]{2,1,0:T(8,128)(2,1)S(1)}, bf16[2,1536,384]{2,1,0:T(8,128)(2,1)S(1)}, u32[]{:S(2)}, u32[]{:S(2)}) collective-permute-start(bf16[2,1536,384]{2,1,0:T(8,128)(2,1)S(1)} %collective-permute-done.6.refs_1_), channel_id=1, source_target_pairs={{0,8},{2,10},{4,12},{6,14},{8,0},{10,2},{12,4},{14,6},{1,9},{3,11}... | collective-permute-start | bytes 7077896 | tf_op jit(solution)/shard_map/ppermute | solution.py:33
  38.6 0.3 shard_map.77.amp_ref
  38.9 15.0 %collective-permute-done.5.x_ref = bf16[1536,384]{1,0:T(8,128)(2,1)S(1)} collective-permute-done((bf16[1536,384]{1,0:T(8,128)(2,1)S(1)}, bf16[1536,384]{1,0:T(8,128)(2,1)S(1)}, u32[]{:S(2)}, u32[]{:S(2)}) %collective-permute-start.5) | collective-permute-done | bytes 1179680 | tf_op jit(solution)/shard_map/ppermute | solution.py:33
  53.9 2.9 %shard_map.78 = (bf16[384,1536]{1,0:T(8,128)(2,1)S(1)}, bf16[2,8,96,384]{3,2,1,0:T(8,128)(2,1)S(1)}) custom-call(s32[16]{0:T(128)S(1)} %stack.80.info, bf16[1536,384]{1,0:T(8,128)(2,1)S(1)} %collective-permute-done.5.x_ref, bf16[1,1500,1500]{2,1,0:T(8,128)(2,1)S(1)} %shard_map.77.amp_ref), custom_call_target="tpu_custom_call" | custom-call | flops 10000000000 | bytes 10000001 | tf_op jit(solution)/shard_map/pallas_call | solution.py:53
  56.8 1.3 %collective-permute-done.3.first_ref.refs_7_ = bf16[2,384,768]{2,1,0:T(8,128)(2,1)S(1)} collective-permute-done((bf16[2,384,768]{2,1,0:T(8,128)(2,1)S(1)}, bf16[2,384,768]{2,1,0:T(8,128)(2,1)S(1)}, u32[]{:S(2)}, u32[]{:S(2)}) %collective-permute-start.3) | collective-permute-done | bytes 1179680 | tf_op jit(solution)/shard_map/ppermute | solution.py:33
  58.0 0.0 collective-permute-done.4.second_ref.refs_6_
  58.1 0.0 collective-permute-done.8.refs_3_
  58.1 0.0 collective-permute-start.9
  58.1 0.6 shard_map.79
  58.7 1.6 %collective-permute-start.10 = (bf16[2,384,768]{2,1,0:T(8,128)(2,1)S(1)}, bf16[2,384,768]{2,1,0:T(8,128)(2,1)S(1)}, u32[]{:S(2)}, u32[]{:S(2)}) collective-permute-start(bf16[2,384,768]{2,1,0:T(8,128)(2,1)S(1)} %shard_map.79), channel_id=1, source_target_pairs={{0,2},{2,4},{4,6},{6,0},{8,14},{10,8},{12,10},{14,12},{1,3},{3,5},... | collective-permute-start | bytes 3538952 | tf_op jit(solution)/shard_map/ppermute | solution.py:33
  60.4 0.6 collective-permute-done.9.refs_4_
  60.9 0.0 collective-permute-done.7.refs_2_
  60.9 15.4 %shard_map.80.refs_6_.early_ref = f32[768,1536]{1,0:T(8,128)S(1)} custom-call(s32[16]{0:T(128)S(1)} %stack.80.info, bf16[384,1536]{1,0:T(8,128)(2,1)S(1)} %get-tuple-element.49.h0_ref, bf16[384,1536]{1,0:T(8,128)(2,1)S(1)} %get-tuple-element.59.h1_ref, bf16[2,1536,384]{2,1,0:T(8,128)(2,1)} %get-tuple-element.54.refs_0_, ...), custom_call_target="tpu_custom_call" | custom-call | flops 1 | bytes 1 | tf_op jit(solution)/shard_map/pallas_call | solution.py:53
  76.4 5.8 %shard_map.81 = (bf16[768,768]{1,0:T(8,128)(2,1)S(1)}, bf16[1536,768]{1,0:T(8,128)(2,1)S(1)}, bf16[768,768]{1,0:T(8,128)(2,1)S(1)}, bf16[768,768]{1,0:T(8,128)(2,1)S(1)}, bf16[8,96,768]{2,1,0:T(8,128)(2,1)S(1)}) custom-call(s32[16]{0:T(128)S(1)} %stack.80.info, bf16[384,1536]{1,0:T(8,128)(2,1)S(1)} %get-tuple-element.49.h0_ref, ...), custom_call_target="tpu_custom_call" | custom-call | flops 1 | bytes 1 | tf_op jit(solution)/shard_map/pallas_call | solution.py:53
  82.1 1.2 collective-permute-start.11
  83.3 2.9 %shard_map.84 = (bf16[768,768]{1,0:T(8,128)(2,1)S(1)}, bf16[768,768]{1,0:T(8,128)(2,1)S(1)}) custom-call(f32[768,1536]{1,0:T(8,128)S(1)} %shard_map.80.refs_6_.early_ref, bf16[768,768]{1,0:T(8,128)(2,1)S(1)} %get-tuple-element.70.newest_ref, bf16[1536,768]{1,0:T(8,128)(2,1)S(1)} %get-tuple-element.71.xn_ref, ...), custom_call_target="tpu_custom_call" | custom-call | flops 1 | bytes 1 | tf_op jit(solution)/shard_map/pallas_call | solution.py:53
  86.3 0.3 collective-permute-start.13
  86.6 0.0 collective-permute-done.11.got_ref
  86.6 1.1 shard_map.82
  87.7 3.5 %collective-permute-start.12 = (bf16[384,768]{1,0:T(8,128)(2,1)S(1)}, bf16[384,768]{1,0:T(8,128)(2,1)S(1)}, u32[]{:S(2)}, u32[]{:S(2)}) collective-permute-start(bf16[384,768]{1,0:T(8,128)(2,1)S(1)} %get-tuple-element.68), channel_id=1, source_target_pairs={{0,16},{2,18},{4,20},{6,22},{8,24},{10,26},{12,28},{14,30},{1,17},... | collective-permute-start | bytes 1769480 | tf_op jit(solution)/shard_map/ppermute | solution.py:33
  91.2 0.0 collective-permute-done.13.got_ref
  91.2 1.1 shard_map.85
  92.3 0.0 copy-start.3
  92.3 0.1 collective-permute-start.14
  92.4 1.6 %collective-permute-start.15 = (bf16[2,96,768]{2,1,0:T(8,128)(2,1)S(1)}, bf16[2,96,768]{2,1,0:T(8,128)(2,1)S(1)}, u32[]{:S(2)}, u32[]{:S(2)}) collective-permute-start(bf16[2,96,768]{2,1,0:T(8,128)(2,1)S(1)} %get-tuple-element.75), channel_id=1, source_target_pairs={{0,32},{2,34},{4,36},{6,38},{8,40},{10,42},{12,44},{14,46},{1,33},... | collective-permute-start | bytes 884744 | tf_op jit(solution)/shard_map/ppermute | solution.py:33
  93.9 1.8 %collective-permute-start.16 = (bf16[2,96,768]{2,1,0:T(8,128)(2,1)S(1)}, bf16[2,96,768]{2,1,0:T(8,128)(2,1)S(1)}, u32[]{:S(2)}, u32[]{:S(2)}) collective-permute-start(bf16[2,96,768]{2,1,0:T(8,128)(2,1)S(1)} %get-tuple-element.76), channel_id=1, source_target_pairs={{0,96},{2,98},{4,100},{6,102},{8,104},{10,106},{12,108},{14,110},{... | collective-permute-start | bytes 884744 | tf_op jit(solution)/shard_map/ppermute | solution.py:33
  95.7 9.5 %collective-permute-done.12.got_ref = bf16[384,768]{1,0:T(8,128)(2,1)S(1)} collective-permute-done((bf16[384,768]{1,0:T(8,128)(2,1)S(1)}, bf16[384,768]{1,0:T(8,128)(2,1)S(1)}, u32[]{:S(2)}, u32[]{:S(2)}) %collective-permute-start.12) | collective-permute-done | bytes 589856 | tf_op jit(solution)/shard_map/ppermute | solution.py:33
  105.2 0.1 shard_map.83
  105.3 0.4 collective-permute-start.17
  105.6 1.7 %collective-permute-start.18 = (bf16[96,768]{1,0:T(8,128)(2,1)S(1)}, bf16[96,768]{1,0:T(8,128)(2,1)S(1)}, u32[]{:S(2)}, u32[]{:S(2)}) collective-permute-start(bf16[96,768]{1,0:T(8,128)(2,1)S(1)} %get-tuple-element.79), channel_id=1, source_target_pairs={{0,32},{2,34},{4,36},{6,38},{8,40},{10,42},{12,44},{14,46},{1,33},... | collective-permute-start | bytes 442376 | tf_op jit(solution)/shard_map/ppermute | solution.py:33
  107.3 1.6 %collective-permute-start.19 = (bf16[96,768]{1,0:T(8,128)(2,1)S(1)}, bf16[96,768]{1,0:T(8,128)(2,1)S(1)}, u32[]{:S(2)}, u32[]{:S(2)}) collective-permute-start(bf16[96,768]{1,0:T(8,128)(2,1)S(1)} %get-tuple-element.80), channel_id=1, source_target_pairs={{0,96},{2,98},{4,100},{6,102},{8,104},{10,106},{12,108},{14,110},{... | collective-permute-start | bytes 442376 | tf_op jit(solution)/shard_map/ppermute | solution.py:33
  109.6 0.1 pad_add_fusion.numbers
  109.6 0.0 collective-permute-done.15.got_2
  109.6 0.0 collective-permute-done.16.got_3
  109.7 0.1 shard_map.87
  109.8 0.0 copy-start.2
  109.8 3.1 %collective-permute-start.20 = (bf16[96,768]{1,0:T(8,128)(2,1)S(1)}, bf16[96,768]{1,0:T(8,128)(2,1)S(1)}, u32[]{:S(2)}, u32[]{:S(2)}) collective-permute-start(bf16[96,768]{1,0:T(8,128)(2,1)S(1)} %get-tuple-element.86), channel_id=1, source_target_pairs={{0,16},{2,18},{4,20},{6,22},{8,24},{10,26},{12,28},{14,30},{1,17},... | collective-permute-start | bytes 442376 | tf_op jit(solution)/shard_map/ppermute | solution.py:33
  112.9 0.7 collective-permute-done.17.refs_0_
  113.6 1.8 %collective-permute-done.18.refs_1_ = bf16[96,768]{1,0:T(8,128)(2,1)S(1)} collective-permute-done((bf16[96,768]{1,0:T(8,128)(2,1)S(1)}, bf16[96,768]{1,0:T(8,128)(2,1)S(1)}, u32[]{:S(2)}, u32[]{:S(2)}) %collective-permute-start.18) | collective-permute-done | bytes 147488 | tf_op jit(solution)/shard_map/ppermute | solution.py:33
  115.4 0.1 shard_map.86.a_ref
  115.5 1.0 collective-permute-done.20.b1_ref
  116.5 0.9 shard_map.88
  117.4 0.9 reshape.11
  118.4 0.8 slice.9
  (13 shorter events, 0.0 us)
Async XLA Ops:
  0.0 3.0 %copy-start.1 = (bf16[1500,375]{1,0:T(8,128)(2,1)S(1)}, bf16[1500,375]{1,0:T(8,128)(2,1)}, u32[]{:S(2)}) copy-start(bf16[1500,375]{1,0:T(8,128)(2,1)} %own_ref.1) | copy-start | bytes 3375004
  0.0 3.0 %collective-permute-start.2 = (bf16[1500,375]{1,0:T(8,128)(2,1)}, bf16[1500,375]{1,0:T(8,128)(2,1)S(1)}, u32[]{:S(2)}, u32[]{:S(2)}) collective-permute-start(bf16[1500,375]{1,0:T(8,128)(2,1)} %own_ref.1), channel_id=1, source_target_pairs={{0,8},{2,10},{4,12},{6,14},{8,0},{10,2},{12,4},{14,6},{1,9},{3,11}... | collective-permute-start | bytes 3375008 | tf_op jit(solution)/shard_map/ppermute | solution.py:33
  4.9 31.2 %collective-permute-start.6 = (bf16[2,1536,384]{2,1,0:T(8,128)(2,1)}, bf16[2,1536,384]{2,1,0:T(8,128)(2,1)S(1)}, u32[]{:S(2)}, u32[]{:S(2)}) collective-permute-start(bf16[2,1536,384]{2,1,0:T(8,128)(2,1)} %get-tuple-element.54.refs_0_), channel_id=1, source_target_pairs={{0,32},{2,34},{4,36},{6,38},{8,104},{10,106},{12,108},{14,110},{1,... | collective-permute-start | bytes 7077896 | tf_op jit(solution)/shard_map/ppermute | solution.py:33
  6.9 16.9 %collective-permute-start = (bf16[384,768]{1,0:T(8,128)(2,1)}, bf16[384,768]{1,0:T(8,128)(2,1)}, u32[]{:S(2)}, u32[]{:S(2)}) collective-permute-start(bf16[384,768]{1,0:T(8,128)(2,1)} %shard_map.73.own_ref), channel_id=1, source_target_pairs={{0,1},{2,3},{4,5},{6,7},{8,9},{10,11},{12,13},{14,15},{1,17},{3,19... | collective-permute-start | bytes 1769480 | tf_op jit(solution)/shard_map/ppermute | solution.py:33
  8.4 15.4 %collective-permute-start.1 = (bf16[384,768]{1,0:T(8,128)(2,1)}, bf16[384,768]{1,0:T(8,128)(2,1)}, u32[]{:S(2)}, u32[]{:S(2)}) collective-permute-start(bf16[384,768]{1,0:T(8,128)(2,1)} %shard_map.73.own_ref), channel_id=1, source_target_pairs={{1,16},{3,18},{5,20},{7,22},{9,24},{11,26},{13,28},{15,30},{16,1},... | collective-permute-start | bytes 1769480 | tf_op jit(solution)/shard_map/ppermute | solution.py:33
  10.0 2.3 %copy-start = (bf16[1,1500,1500]{2,1,0:T(8,128)(2,1)S(1)}, bf16[1,1500,1500]{2,1,0:T(8,128)(2,1)}, u32[]{:S(2)}) copy-start(bf16[1,1500,1500]{2,1,0:T(8,128)(2,1)} %in_ref) | copy-start | bytes 13500004
  23.8 14.8 %slice-start = ((s8[4620288]{0:T(1024)(128)(4,1)}), s8[4194304]{0:T(1024)(128)(4,1)S(1)}, s32[]{:S(2)}) async-start(s8[4620288]{0:T(1024)(128)(4,1)} %bitcast.20), calls=%async_computation | async-start | bytes 8388608
  23.8 14.8 %slice-start.1 = ((s8[4620288]{0:T(1024)(128)(4,1)}), s8[425984]{0:T(1024)(128)(4,1)S(1)}, s32[]{:S(2)}) async-start(s8[4620288]{0:T(1024)(128)(4,1)} %bitcast.20), calls=%async_computation.1 | async-start | bytes 851968
  23.8 30.1 %collective-permute-start.5 = (bf16[1536,384]{1,0:T(8,128)(2,1)S(1)}, bf16[1536,384]{1,0:T(8,128)(2,1)S(1)}, u32[]{:S(2)}, u32[]{:S(2)}) collective-permute-start(bf16[1536,384]{1,0:T(8,128)(2,1)S(1)} %get-tuple-element.53.x_ref), channel_id=1, source_target_pairs={{0,17},{2,19},{4,21},{6,23},{8,25},{10,27},{12,29},{14,31},{1,16},... | collective-permute-start | bytes 3538952 | tf_op jit(solution)/shard_map/ppermute | solution.py:33
  28.1 29.9 %collective-permute-start.3 = (bf16[2,384,768]{2,1,0:T(8,128)(2,1)S(1)}, bf16[2,384,768]{2,1,0:T(8,128)(2,1)S(1)}, u32[]{:S(2)}, u32[]{:S(2)}) collective-permute-start(bf16[2,384,768]{2,1,0:T(8,128)(2,1)S(1)} %shard_map.76.refs_5_), channel_id=1, source_target_pairs={{0,2},{2,4},{4,6},{6,0},{8,10},{10,12},{12,14},{14,8},{1,3},{3,5},... | collective-permute-start | bytes 3538952 | tf_op jit(solution)/shard_map/ppermute | solution.py:33
  29.8 28.3 %collective-permute-start.4 = (bf16[2,384,768]{2,1,0:T(8,128)(2,1)S(1)}, bf16[2,384,768]{2,1,0:T(8,128)(2,1)S(1)}, u32[]{:S(2)}, u32[]{:S(2)}) collective-permute-start(bf16[2,384,768]{2,1,0:T(8,128)(2,1)S(1)} %shard_map.76.refs_5_), channel_id=1, source_target_pairs={{0,6},{2,0},{4,2},{6,4},{8,14},{10,8},{12,10},{14,12},{1,7},{3,1},... | collective-permute-start | bytes 3538952 | tf_op jit(solution)/shard_map/ppermute | solution.py:33
  36.2 21.9 %collective-permute-start.8 = (bf16[1536,384]{1,0:T(8,128)(2,1)S(1)}, bf16[1536,384]{1,0:T(8,128)(2,1)S(1)}, u32[]{:S(2)}, u32[]{:S(2)}) collective-permute-start(bf16[1536,384]{1,0:T(8,128)(2,1)S(1)} %slice_bitcast_fusion), channel_id=1, source_target_pairs={{0,32},{2,34},{4,36},{6,38},{8,104},{10,106},{12,108},{14,110},{1,... | collective-permute-start | bytes 3538952 | tf_op jit(solution)/shard_map/ppermute | solution.py:33
  36.3 24.7 %collective-permute-start.7 = (bf16[2,1536,384]{2,1,0:T(8,128)(2,1)S(1)}, bf16[2,1536,384]{2,1,0:T(8,128)(2,1)S(1)}, u32[]{:S(2)}, u32[]{:S(2)}) collective-permute-start(bf16[2,1536,384]{2,1,0:T(8,128)(2,1)S(1)} %collective-permute-done.6.refs_1_), channel_id=1, source_target_pairs={{0,8},{2,10},{4,12},{6,14},{8,0},{10,2},{12,4},{14,6},{1,9},{3,11}... | collective-permute-start | bytes 7077896 | tf_op jit(solution)/shard_map/ppermute | solution.py:33
  58.1 2.8 %collective-permute-start.9 = (bf16[1536,384]{1,0:T(8,128)(2,1)S(1)}, bf16[1536,384]{1,0:T(8,128)(2,1)S(1)}, u32[]{:S(2)}, u32[]{:S(2)}) collective-permute-start(bf16[1536,384]{1,0:T(8,128)(2,1)S(1)} %collective-permute-done.8.refs_3_), channel_id=1, source_target_pairs={{0,8},{2,10},{4,12},{6,14},{8,0},{10,2},{12,4},{14,6},{1,9},{3,11}... | collective-permute-start | bytes 3538952 | tf_op jit(solution)/shard_map/ppermute | solution.py:33
  58.7 17.6 %collective-permute-start.10 = (bf16[2,384,768]{2,1,0:T(8,128)(2,1)S(1)}, bf16[2,384,768]{2,1,0:T(8,128)(2,1)S(1)}, u32[]{:S(2)}, u32[]{:S(2)}) collective-permute-start(bf16[2,384,768]{2,1,0:T(8,128)(2,1)S(1)} %shard_map.79), channel_id=1, source_target_pairs={{0,2},{2,4},{4,6},{6,0},{8,14},{10,8},{12,10},{14,12},{1,3},{3,5},... | collective-permute-start | bytes 3538952 | tf_op jit(solution)/shard_map/ppermute | solution.py:33
  82.1 4.4 %collective-permute-start.11 = (bf16[768,768]{1,0:T(8,128)(2,1)S(1)}, bf16[768,768]{1,0:T(8,128)(2,1)S(1)}, u32[]{:S(2)}, u32[]{:S(2)}) collective-permute-start(bf16[768,768]{1,0:T(8,128)(2,1)S(1)} %get-tuple-element.66), channel_id=1, source_target_pairs={{0,8},{2,10},{4,12},{6,14},{8,0},{10,2},{12,4},{14,6},{1,9},{3,11}... | collective-permute-start | bytes 3538952 | tf_op jit(solution)/shard_map/ppermute | solution.py:33
  86.3 4.9 %collective-permute-start.13 = (bf16[768,768]{1,0:T(8,128)(2,1)S(1)}, bf16[768,768]{1,0:T(8,128)(2,1)S(1)}, u32[]{:S(2)}, u32[]{:S(2)}) collective-permute-start(bf16[768,768]{1,0:T(8,128)(2,1)S(1)} %get-tuple-element.73), channel_id=1, source_target_pairs={{0,8},{2,10},{4,12},{6,14},{8,0},{10,2},{12,4},{14,6},{1,9},{3,11}... | collective-permute-start | bytes 3538952 | tf_op jit(solution)/shard_map/ppermute | solution.py:33
  87.7 17.5 %collective-permute-start.12 = (bf16[384,768]{1,0:T(8,128)(2,1)S(1)}, bf16[384,768]{1,0:T(8,128)(2,1)S(1)}, u32[]{:S(2)}, u32[]{:S(2)}) collective-permute-start(bf16[384,768]{1,0:T(8,128)(2,1)S(1)} %get-tuple-element.68), channel_id=1, source_target_pairs={{0,16},{2,18},{4,20},{6,22},{8,24},{10,26},{12,28},{14,30},{1,17},... | collective-permute-start | bytes 1769480 | tf_op jit(solution)/shard_map/ppermute | solution.py:33
  92.3 17.2 %copy-start.3 = (f32[1500]{0:T(1024)S(1)}, f32[1500]{0:T(1024)}, u32[]{:S(2)}) copy-start(f32[1500]{0:T(1024)} %param.12) | copy-start | bytes 18004
  92.3 15.0 %collective-permute-start.14 = (bf16[2,96,768]{2,1,0:T(8,128)(2,1)S(1)}, bf16[2,96,768]{2,1,0:T(8,128)(2,1)S(1)}, u32[]{:S(2)}, u32[]{:S(2)}) collective-permute-start(bf16[2,96,768]{2,1,0:T(8,128)(2,1)S(1)} %get-tuple-element.74), channel_id=1, source_target_pairs={{0,64},{2,66},{4,68},{6,70},{8,72},{10,74},{12,76},{14,78},{1,65},... | collective-permute-start | bytes 884744 | tf_op jit(solution)/shard_map/ppermute | solution.py:33
  92.4 17.3 %collective-permute-start.15 = (bf16[2,96,768]{2,1,0:T(8,128)(2,1)S(1)}, bf16[2,96,768]{2,1,0:T(8,128)(2,1)S(1)}, u32[]{:S(2)}, u32[]{:S(2)}) collective-permute-start(bf16[2,96,768]{2,1,0:T(8,128)(2,1)S(1)} %get-tuple-element.75), channel_id=1, source_target_pairs={{0,32},{2,34},{4,36},{6,38},{8,40},{10,42},{12,44},{14,46},{1,33},... | collective-permute-start | bytes 884744 | tf_op jit(solution)/shard_map/ppermute | solution.py:33
  93.9 15.7 %collective-permute-start.16 = (bf16[2,96,768]{2,1,0:T(8,128)(2,1)S(1)}, bf16[2,96,768]{2,1,0:T(8,128)(2,1)S(1)}, u32[]{:S(2)}, u32[]{:S(2)}) collective-permute-start(bf16[2,96,768]{2,1,0:T(8,128)(2,1)S(1)} %get-tuple-element.76), channel_id=1, source_target_pairs={{0,96},{2,98},{4,100},{6,102},{8,104},{10,106},{12,108},{14,110},{... | collective-permute-start | bytes 884744 | tf_op jit(solution)/shard_map/ppermute | solution.py:33
  105.3 8.3 %collective-permute-start.17 = (bf16[96,768]{1,0:T(8,128)(2,1)S(1)}, bf16[96,768]{1,0:T(8,128)(2,1)S(1)}, u32[]{:S(2)}, u32[]{:S(2)}) collective-permute-start(bf16[96,768]{1,0:T(8,128)(2,1)S(1)} %get-tuple-element.78), channel_id=1, source_target_pairs={{0,64},{2,66},{4,68},{6,70},{8,72},{10,74},{12,76},{14,78},{1,65},... | collective-permute-start | bytes 442376 | tf_op jit(solution)/shard_map/ppermute | solution.py:33
  105.6 9.8 %collective-permute-start.18 = (bf16[96,768]{1,0:T(8,128)(2,1)S(1)}, bf16[96,768]{1,0:T(8,128)(2,1)S(1)}, u32[]{:S(2)}, u32[]{:S(2)}) collective-permute-start(bf16[96,768]{1,0:T(8,128)(2,1)S(1)} %get-tuple-element.79), channel_id=1, source_target_pairs={{0,32},{2,34},{4,36},{6,38},{8,40},{10,42},{12,44},{14,46},{1,33},... | collective-permute-start | bytes 442376 | tf_op jit(solution)/shard_map/ppermute | solution.py:33
  107.3 8.1 %collective-permute-start.19 = (bf16[96,768]{1,0:T(8,128)(2,1)S(1)}, bf16[96,768]{1,0:T(8,128)(2,1)S(1)}, u32[]{:S(2)}, u32[]{:S(2)}) collective-permute-start(bf16[96,768]{1,0:T(8,128)(2,1)S(1)} %get-tuple-element.80), channel_id=1, source_target_pairs={{0,96},{2,98},{4,100},{6,102},{8,104},{10,106},{12,108},{14,110},{... | collective-permute-start | bytes 442376 | tf_op jit(solution)/shard_map/ppermute | solution.py:33
  109.8 6.7 %copy-start.2 = (f32[150]{0:T(256)S(1)}, f32[150]{0:T(256)}, u32[]{:S(2)}) copy-start(f32[150]{0:T(256)} %param.13) | copy-start | bytes 1804
  109.8 6.7 %collective-permute-start.20 = (bf16[96,768]{1,0:T(8,128)(2,1)S(1)}, bf16[96,768]{1,0:T(8,128)(2,1)S(1)}, u32[]{:S(2)}, u32[]{:S(2)}) collective-permute-start(bf16[96,768]{1,0:T(8,128)(2,1)S(1)} %get-tuple-element.86), channel_id=1, source_target_pairs={{0,16},{2,18},{4,20},{6,22},{8,24},{10,26},{12,28},{14,30},{1,17},... | collective-permute-start | bytes 442376 | tf_op jit(solution)/shard_map/ppermute | solution.py:33
